TPU v7x, 512 devices: a whole 4x8x8 slice. The times are simulated.
512 devices in a mesh: dp: 64 (over y, z_lo, core), proto: 8 (over z_hi, x).
Axes of the slice: x: 4, y: 8, z: 8 (z_hi: 2, z_lo: 4; z = z_hi * 4 + z_lo), core: 2. Of those that a mesh axis runs over, the one named last changes fastest.
Arguments:
- tokens: bfloat16 [4096, 32, 128], P('dp'), may hold values from -7 to 7
- offsets: int32 [2, 4096], P(None, 'dp'), may hold values from 0 to 8
- species: int32 [4096], P('dp'), may hold values from 0 to 15
- prototypes: bfloat16 [65536, 128], P('proto'), may hold values from -2 to 2
Outputs:
- view_grads: float32 [2, 4096, 128], P(None, 'dp')
- proto_grads: float32 [65536, 128], P(('proto', 'dp'))
- loss: float32 [], replicated
Inputs may be any that keep to these rules, and one draw needn't show every extreme that they name: `offsets`: the start of a view's pooled positions within its window.
All inputs are finite; a program needn't handle non-finite values.
Results may differ from a plain program's by a relative error of at most 0.011.
The roundings to bfloat16 on the way count: a program that leaves them out, or rounds other values in their place, can miss the bound.
Values sent between devices are 32-bit elements; how exact they have to be, the bound alone decides.
A program may use at most 64 MiB of HBM per device.

v0:
```python
import math

import jax
import jax.numpy as jnp
from jax import lax
from jax.sharding import PartitionSpec as P

NGROUP = 16
CROP = 24
ITERS = 3


peaking_denominator = 0.1
entropic = 0.05


def unit_rows(matrix):
    return (
        matrix
        * lax.rsqrt(jnp.mean(matrix * matrix, axis=-1, keepdims=True) + 1e-06)
        / math.sqrt(matrix.shape[-1])
    )


def on_device(tokens, offsets, species, prototypes):
    window_count = tokens.shape[0]
    seq_len = tokens.shape[1]
    feat_width = tokens.shape[2]
    local_keys = prototypes.shape[0]
    proto_devices = lax.axis_size("proto")
    data_devices = lax.axis_size("dp")
    windows = window_count * data_devices
    key_total = local_keys * proto_devices
    position = jnp.arange(seq_len, dtype=jnp.int32)
    starts = offsets[:, :, None]
    window_mask = ((position >= starts) & (position < starts + CROP)).astype(jnp.bfloat16)
    pooled = (
        jnp.einsum("vwt,wtf->vwf", window_mask, tokens, preferred_element_type=jnp.float32) / CROP
    )
    unit_views, back_views = jax.vjp(unit_rows, pooled)
    queries = unit_views.astype(jnp.bfloat16)
    unit_keys = unit_rows(prototypes.astype(jnp.float32)).astype(jnp.bfloat16)
    cosine_match_matrix = lax.dot_general(
        queries, unit_keys, (((2,), (1,)), ((), ())), preferred_element_type=jnp.float32
    )
    kernel_vals = jnp.exp(cosine_match_matrix / entropic).astype(jnp.bfloat16)
    onehot = (species[:, None] == jnp.arange(NGROUP, dtype=jnp.int32)).astype(jnp.float32)
    local_counts = jnp.sum(onehot, axis=0)

    def row_scaling(proto_scale):
        local_sums = jnp.sum(kernel_vals.astype(jnp.float32) * proto_scale[:, None, :], axis=2)
        return 1.0 / lax.psum(local_sums, "proto")

    proto_scale = jnp.full((2, local_keys), 1.0 / key_total, jnp.float32)
    for sweep_index in range(ITERS):
        window_scale = row_scaling(proto_scale)
        local_sums = jnp.sum(kernel_vals.astype(jnp.float32) * window_scale[:, :, None], axis=1)
        if sweep_index == ITERS - 1:
            counts = lax.psum(local_counts, "dp")
            columns = lax.psum(local_sums, "dp")
        else:
            columns = lax.psum(local_sums, "dp")
        proto_scale = 1.0 / (key_total * columns)
    window_scale = row_scaling(proto_scale)
    assigned = kernel_vals.astype(jnp.float32) * proto_scale[:, None, :] * window_scale[:, :, None]
    unscaled_anchor_closeness = cosine_match_matrix / peaking_denominator
    logarithmic_normalizer = jnp.log(
        lax.psum(jnp.sum(jnp.exp(unscaled_anchor_closeness), axis=2), "proto")
    )
    guessed_label_share = jnp.exp(unscaled_anchor_closeness - logarithmic_normalizer[:, :, None])
    crossed_label_aim = assigned[::-1]
    crossed = jnp.sum(crossed_label_aim * unscaled_anchor_closeness, axis=2)
    prototype_weight = windows / (NGROUP * jnp.sum(onehot * counts[None, :], axis=1))
    partial_loss = (
        jnp.sum(
            prototype_weight * jnp.sum(logarithmic_normalizer / proto_devices - crossed, axis=0)
        )
        / 2.0
    )
    summed = lax.psum(partial_loss, ("dp", "proto"))
    kinship_slope = (
        prototype_weight[None, :, None]
        / (2.0 * peaking_denominator)
        * (guessed_label_share - crossed_label_aim)
    ).astype(jnp.bfloat16)
    flat_grad = kinship_slope.reshape(2 * window_count, local_keys)
    flat_queries = queries.reshape(2 * window_count, feat_width)
    rows_each = local_keys // data_devices
    key_term_full = lax.dot_general(
        flat_grad, flat_queries, (((0,), (0,)), ((), ())), preferred_element_type=jnp.float32
    )
    key_grad = lax.psum_scatter(key_term_full, "dp", scatter_dimension=0, tiled=True)
    query_part = lax.dot_general(
        kinship_slope, unit_keys, (((2,), (0,)), ((), ())), preferred_element_type=jnp.float32
    )
    query_grad = lax.psum(query_part, "proto")
    view_grads = back_views(query_grad)[0]
    own_rows = lax.dynamic_slice_in_dim(
        prototypes, lax.axis_index("dp") * rows_each, rows_each, 0
    ).astype(jnp.float32)
    own_unit, back_own = jax.vjp(unit_rows, own_rows)
    proto_grads = back_own(key_grad)[0]
    return (view_grads, proto_grads, summed / windows)


def solution(mesh):
    return jax.shard_map(
        on_device,
        mesh=mesh,
        in_specs=(P("dp", None, None), P(None, "dp"), P("dp"), P("proto", None)),
        out_specs=(P(None, "dp", None), P(("proto", "dp"), None), P()),
        check_vma=False,
    )
```

profile of v0, /device:TPU:1, one launch (start us, length us, event | category | flops | bytes accessed | tf_op | source)
XLA Modules:
  0.0 1956.9 jit_solution(13193151728101666574)
XLA Ops:
  7.2 0.0 copy-start
  7.2 0.0 all-reduce.5.cloned.1.call-start
  7.2 0.7 broadcast_add_fusion
  8.0 0.8 copy.19
  8.7 0.1 copy.20
  8.8 0.0 copy-done
  8.8 0.3 fusion.16
  9.1 0.1 multiply_reduce_fusion.2
  9.3 2.8 fusion.2
  12.0 4.6 fusion.5
  16.6 0.0 copy-start.4
  16.6 32.2 %psum.79 = f32[2,64]{1,0:T(2,128)S(1)} all-reduce(f32[2,64]{1,0:T(2,128)S(1)} %get-tuple-element.15), channel_id=1, replica_groups=mesh['dp'=64,'proto'=8] {'proto'}, use_global_device_ids=true, to_apply=%region_8.0 | all-reduce | flops 128 | bytes 1024 | tf_op jit(solution)/shard_map/psum | solution.py:52
  48.8 1.2 fusion.6
  50.0 0.0 all-reduce.5.cloned.1.call-update
  50.1 0.0 all-reduce.7.cloned.1.call-start
  50.1 462.2 %all-reduce.5.cloned.1.call-done = f32[2,8192]{1,0:T(2,128)} async-done(((f32[2,8192]{1,0:T(2,128)}), f32[2,8192]{1,0:T(2,128)}) %all-reduce.5.cloned.1.call-update) | async-done | bytes 65552 | tf_op jit(solution)/shard_map/psum | solution.py:62
  512.3 0.9 multiply_divide_fusion.2
  513.2 0.6 fusion.7
  513.7 26.8 %psum.81 = f32[2,64]{1,0:T(2,128)S(1)} all-reduce(f32[2,64]{1,0:T(2,128)S(1)} %fusion.7), channel_id=1, replica_groups=mesh['dp'=64,'proto'=8] {'proto'}, use_global_device_ids=true, to_apply=%region_12.0 | all-reduce | flops 128 | bytes 1024 | tf_op jit(solution)/shard_map/psum | solution.py:52
  540.6 1.2 fusion.8
  541.8 0.0 all-reduce.7.cloned.1.call-update
  541.8 0.0 all-reduce.9.cloned.1.call-start
  541.9 0.0 copy-done.4
  541.9 0.1 convert_reduce_fusion
  542.0 141.4 %psum.77 = f32[16]{0:T(128)S(1)} all-reduce(f32[16]{0:T(128)S(1)} %convert_reduce_fusion), channel_id=1, replica_groups=mesh['dp'=64,'proto'=8] {'dp'}, use_global_device_ids=true, to_apply=%region_1.0 | all-reduce | flops 16 | bytes 128 | tf_op jit(solution)/shard_map/psum | solution.py:59
  683.4 318.6 %all-reduce.7.cloned.1.call-done = f32[2,8192]{1,0:T(2,128)} async-done(((f32[2,8192]{1,0:T(2,128)}), f32[2,8192]{1,0:T(2,128)}) %all-reduce.7.cloned.1.call-update) | async-done | bytes 65552 | tf_op jit(solution)/shard_map/psum | solution.py:62
  1002.0 0.9 multiply_divide_fusion.1
  1002.9 0.6 fusion.9
  1003.5 26.8 %psum.83 = f32[2,64]{1,0:T(2,128)S(1)} all-reduce(f32[2,64]{1,0:T(2,128)S(1)} %fusion.9), channel_id=1, replica_groups=mesh['dp'=64,'proto'=8] {'proto'}, use_global_device_ids=true, to_apply=%region_16.0 | all-reduce | flops 128 | bytes 1024 | tf_op jit(solution)/shard_map/psum | solution.py:52
  1030.3 1.2 fusion.10
  1031.5 0.0 all-reduce.9.cloned.1.call-update
  1031.6 0.0 all-reduce.11.cloned.1.call-start
  1031.6 0.1 select_reduce_fusion
  1031.7 460.0 %all-reduce.9.cloned.1.call-done = f32[2,8192]{1,0:T(2,128)} async-done(((f32[2,8192]{1,0:T(2,128)}), f32[2,8192]{1,0:T(2,128)}) %all-reduce.9.cloned.1.call-update) | async-done | bytes 65552 | tf_op jit(solution)/shard_map/psum | solution.py:60
  1491.7 0.9 multiply_divide_fusion
  1492.6 0.5 fusion.1
  1493.1 26.8 %psum.85 = f32[2,64]{1,0:T(2,128)S(1)} all-reduce(f32[2,64]{1,0:T(2,128)S(1)} %fusion.1), channel_id=1, replica_groups=mesh['dp'=64,'proto'=8] {'proto'}, use_global_device_ids=true, to_apply=%region_20.0 | all-reduce | flops 128 | bytes 1024 | tf_op jit(solution)/shard_map/psum | solution.py:52
  1520.0 0.0 copy-start.1
  1520.0 0.6 fusion
  1520.5 0.0 copy-start.2
  1520.6 3.1 copy-done.1
  1523.7 1.2 multiply_reduce_fusion
  1524.9 0.0 copy-done.2
  1524.9 20.3 %psum.78 = f32[2,64]{1,0:T(2,128)S(1)} all-reduce(f32[2,64]{1,0:T(2,128)S(1)} %get-tuple-element.10), channel_id=1, replica_groups=mesh['dp'=64,'proto'=8] {'proto'}, use_global_device_ids=true, to_apply=%region_6.0 | all-reduce | flops 128 | bytes 1024 | tf_op jit(solution)/shard_map/psum | solution.py:68
  1545.2 0.6 multiply_reduce_fusion.3
  1545.9 0.0 copy-start.3
  1545.9 4.6 multiply_convert_fusion
  1550.4 0.0 copy-done.3
  1550.4 2.0 fusion.12
  1552.5 0.0 all-reduce.11.cloned.1.call-update
  1552.5 0.0 reduce-scatter.2.cloned.1.call-start
  1552.5 2.7 convolution_bitcast_fusion
  1555.3 0.0 reduce-scatter.2.cloned.1.call-update
  1555.9 106.2 %psum.87 = f32[]{:T(128)} all-reduce(f32[]{:T(128)S(6)} %div.145), channel_id=1, replica_groups=mesh['dp'=64,'proto'=8] {'dp','proto'}, use_global_device_ids=true, to_apply=%region_29.0 | all-reduce | flops 1 | bytes 8 | tf_op jit(solution)/shard_map/psum | solution.py:80
  1662.8 0.0 all-reduce.11.cloned.1.call-done
  1662.8 0.9 multiply_reduce_fusion.1
  1663.8 1.6 add_add_fusion.1
  1665.3 281.3 %reduce-scatter.2.cloned.1.call-done = f32[128,128]{1,0:T(8,128)} async-done(((f32[8192,128]{1,0:T(8,128)}), f32[128,128]{1,0:T(8,128)}) %reduce-scatter.2.cloned.1.call-update) | async-done | bytes 65552 | tf_op jit(solution)/shard_map/reduce_scatter | solution.py:92
  1946.7 1.0 fusion.20
  1947.7 1.6 add_add_fusion
  (10 shorter events, 0.1 us)
Async XLA Ops:
  7.2 1.7 copy-start
  7.2 505.1 %all-reduce.5.cloned.1.call-start = ((), (), s32[]{:S(2)}) async-start(), calls=%async_computation.1 | async-start | bytes 131072 | tf_op jit(solution)/shard_map/psum | solution.py:62
  16.6 525.3 %copy-start.4 = (s32[64]{0:T(128)S(1)}, s32[64]{0:T(128)}, u32[]{:S(2)}) copy-start(s32[64]{0:T(128)} %param.6) | copy-start | bytes 772
  50.1 951.9 %all-reduce.7.cloned.1.call-start = ((), (), s32[]{:S(2)}) async-start(), calls=%async_computation.2 | async-start | bytes 131072 | tf_op jit(solution)/shard_map/psum | solution.py:62
  541.8 949.9 %all-reduce.9.cloned.1.call-start = ((), (), s32[]{:S(2)}) async-start(), calls=%async_computation.3 | async-start | bytes 131072 | tf_op jit(solution)/shard_map/psum | solution.py:60
  1031.6 631.2 %all-reduce.11.cloned.1.call-start = ((), (), s32[]{:S(2)}) async-start(), calls=%async_computation.4 | async-start | bytes 131072 | tf_op jit(solution)/shard_map/psum | solution.py:96
  1520.0 3.7 copy-start.1
  1520.5 4.4 copy-start.2
  1545.9 4.6 copy-start.3
  1552.5 394.2 %reduce-scatter.2.cloned.1.call-start = ((), (), s32[]{:S(2)}) async-start(), calls=%async_computation.5 | async-start | bytes 4259840 | tf_op jit(solution)/shard_map/reduce_scatter | solution.py:92
Sparse Core Ops, SparseCore 0:
  50.2 462.0 all-reduce.4
  542.0 459.9 all-reduce.6
  1031.7 459.9 all-reduce.8
  1552.6 109.1 all-reduce.10
  1664.4 282.2 reduce-scatter.1
where the time goes:
time: 1960 us
  waiting for transfers between devices  1520 us (78%)
  blocking collectives  381 us (19%)
  other arithmetic  24 us (1%)
    psum x3, waiting for transfers between devices, on_device(): columns = lax.psum(local_sums, 'dp')  1240 us
    reduce_scatter x1, waiting for transfers between devices, on_device(): lax.psum_scatter(key_term_full, 'dp', scatter_dimension=0, tiled=True)  281 us
    psum x1, blocking collectives, on_device(): counts = lax.psum(local_counts, 'dp')  141 us
    psum x4, blocking collectives, row_scaling(): return 1.0 / lax.psum(local_sums, 'proto')  113 us
    psum x1, blocking collectives, on_device(): summed = lax.psum(partial_loss, ('dp', 'proto'))  106 us
  transfers between devices with their start and end apart: 5, of which 4 were waited for; matrix products, arithmetic and copies ran while one was open for 0% of the time, Pallas kernels for 0%

commit v1 on v0

v1 whole, which is shorter than its diff:
```python
import math

import jax
import jax.numpy as jnp
from jax import lax
from jax.experimental import pallas as pl
from jax.experimental.pallas import tpu as pltpu
from jax.sharding import PartitionSpec as P

MESH = pl.DeviceIdType.MESH
F32 = jnp.float32
BF16 = jnp.bfloat16
NGROUP = 16
CROP = 24
SEQ = 32
FEAT = 128
WINDOWS = 4096
PROTOS = 65536
EPS = 1e-6
NY, NZL, NC, NZH, NX = 8, 4, 2, 2, 4
NZ = NZH * NZL
RING8 = (4, 3, 5, 2, 6, 1, 7)
XC = ((2, 0), (2, 1), (1, 0), (3, 0), (1, 1), (3, 1), (0, 1))
RING4 = (2, 1, 3)
NT = (((1,), (1,)), ((), ()))
NN = (((1,), (0,)), ((), ()))


def mm(a, b, dims=NN):
    return lax.dot_general(a, b, dims, preferred_element_type=F32)


def split3(row, count=16):
    hi = row.astype(BF16).astype(F32)
    rest = row - hi
    mid = rest.astype(BF16).astype(F32)
    lo = rest - mid
    width = row.shape[1]
    at = lax.broadcasted_iota(jnp.int32, (count, width), 0)
    full = lambda r: jnp.broadcast_to(r, (count, width))
    out = jnp.where(at == 0, full(hi), jnp.where(at == 1, full(mid), jnp.where(at == 2, full(lo), 0.0)))
    return out.astype(BF16)


def unit_scale(rows):
    return lax.rsqrt(jnp.mean(rows * rows, axis=-1, keepdims=True) + EPS)


def unit_back(rows, grad):
    scale = unit_scale(rows)
    along = jnp.mean(rows * grad, axis=-1, keepdims=True)
    return (grad - rows * (along * scale * scale)) * (scale / math.sqrt(FEAT))


def kernel(
    tok_ref, off_ref, spec_ref, proto_ref,
    view_ref, pgrad_ref, loss_ref,
    tok, kraw, keys, keys_t, pooled, qg, q16, s_buf, e_buf, k_buf, t_buf, g_buf,
    a_src, a_xc, a_z, b_src, b_y, z_src, z_xc, z_z, cnt_src, cnt_y,
    kg_src, kg_y, c_src, c_rcv, x_src, x_rcv, w_src, w_rcv, fin, l_xc, l_z, l_y,
    x_rows, qt,
    load_sem, g_ssem, g_rsem, gs_ssem, gs_rsem,
    a_ssem, a_rsem, b_ssem, b_rsem, z_ssem, z_rsem, cnt_ssem, cnt_rsem,
    kg_ssem, kg_rsem, f_ssem, f_rsem, l_ssem, l_rsem,
):
    dp = lax.axis_index("dp")
    pr = lax.axis_index("proto")
    y, zl, c = lax.div(dp, 8), lax.rem(lax.div(dp, 2), 4), lax.rem(dp, 2)
    zh, x = lax.div(pr, 4), lax.rem(pr, 4)
    z = zh * NZL + zl

    def dev(y=y, z=z, c=c, x=x):
        return ((y * NZL + lax.rem(z, NZL)) * NC + c, lax.div(z, NZL) * NX + x)

    xc_ids = [dev(x=lax.rem(x + dx, NX), c=lax.rem(c + dc, NC)) for dx, dc in XC]
    z_of = [lax.rem(z + j, NZ) for j in RING8]
    z_ids = [dev(z=k) for k in z_of]
    y_of = [lax.rem(y + j, NY) for j in RING8]
    y_ids = [dev(y=k) for k in y_of]
    x_of = [lax.rem(x + j, NX) for j in RING4]
    x_ids = [dev(x=k) for k in x_of]
    sib = dev(c=1 - c)

    def remote(src, dst, ssem, rsem, to):
        return pltpu.make_async_remote_copy(
            src_ref=src, dst_ref=dst, send_sem=ssem, recv_sem=rsem, device_id=to, device_id_type=MESH
        )

    def got(ref, sem):
        remote(ref, ref, sem, sem, sib).wait_recv()

    def sent(ref, sem):
        remote(ref, ref, sem, sem, sib).wait_send()

    barrier = pltpu.get_barrier_semaphore()
    load_tok = pltpu.make_async_copy(tok_ref, tok, load_sem.at[0])
    load_key = pltpu.make_async_copy(proto_ref.at[:, zl * NC + c], kraw, load_sem.at[1])
    load_tok.start()
    load_key.start()
    for to in xc_ids + z_ids + y_ids:
        pl.semaphore_signal(barrier, inc=1, device_id=to, device_id_type=MESH)

    off = off_ref[...].astype(F32)
    off_row = jnp.concatenate([off[0:1], off[1:2]], axis=1)
    lane = lax.broadcasted_iota(jnp.int32, (128, 128), 1)
    first = jnp.broadcast_to(off_row, (128, 128)).T.astype(jnp.int32)
    row = lax.broadcasted_iota(jnp.int32, (128, 128), 0)
    first = first + (row & 63) * SEQ
    load_tok.wait()
    total = jnp.zeros((128, FEAT), F32)
    for part in range(4):
        mask = jnp.concatenate(
            [
                jnp.where((lane + col >= first) & (lane + col < first + CROP), 1.0, 0.0).astype(BF16)
                for col in range(part * 512, part * 512 + 512, 128)
            ],
            axis=1,
        )
        total = total + mm(mask, tok[pl.ds(part * 512, 512)])
    rows = total / CROP
    pooled[...] = rows
    query = (rows * unit_scale(rows) / math.sqrt(FEAT)).astype(BF16).astype(F32)
    qg[c, zl, pl.ds(0, 128)] = query
    spec = spec_ref[...].astype(F32)
    both = jnp.concatenate([spec, spec], axis=1)
    half = lax.broadcasted_iota(jnp.int32, (8, 128), 1) // 64
    qg[c, zl, pl.ds(128, 8)] = jnp.where(half == c, jnp.broadcast_to(both, (8, 128)), 0.0)

    pl.semaphore_wait(barrier, 21)
    step2 = 2 + 4 * c
    mine = qg.at[c, zl]
    for i, to in enumerate((dev(z=lax.rem(z + step2, NZ)), dev(z=lax.rem(z + 1, NZ)), dev(z=lax.rem(z + 7, NZ)))):
        remote(mine, mine, g_ssem, g_rsem.at[i], to).start()
    remote(mine, mine, gs_ssem, gs_rsem.at[0], sib).start()

    load_key.wait()
    for i in range(8):
        raw = kraw[i].astype(F32)
        unit = raw * unit_scale(raw) / math.sqrt(FEAT)
        keys[pl.ds(i * 128, 128)] = unit.astype(BF16)
        keys_t[:, pl.ds(i * 128, 128)] = unit.astype(BF16).astype(F32).T.astype(BF16)

    def scores(zp):
        zp128 = pl.multiple_of(zp * 128, 128)
        pair = []
        for v in range(2):
            q = jnp.concatenate([qg[0, zp, pl.ds(v * 64, 64)], qg[1, zp, pl.ds(v * 64, 64)]], axis=0).astype(BF16)
            q16[v, pl.ds(zp128, 128)] = q
            pair.append(q)
        rhs = jnp.concatenate(pair, axis=0)

        def block(kb, sums):
            k0 = pl.multiple_of(kb * 128, 128)
            s = mm(keys[pl.ds(k0, 128)], rhs, NT)
            e = jnp.exp(s * 10.0)
            k = (e * e).astype(BF16)
            for v in range(2):
                at = (v, pl.ds(k0, 128), pl.ds(zp128, 128))
                s_buf[at] = s[:, v * 128 : v * 128 + 128]
                e_buf[at] = e[:, v * 128 : v * 128 + 128]
                k_buf[at] = k[:, v * 128 : v * 128 + 128]
            fold = lambda a: jnp.sum(a.reshape(16, 8, 256), axis=0)
            return sums[0] + fold(e), sums[1] + fold(k.astype(F32))

        zero = jnp.zeros((8, 256), F32)
        es, ks = lax.fori_loop(0, 8, block, (zero, zero))
        es = jnp.sum(es, axis=0, keepdims=True)
        ks = jnp.sum(ks, axis=0, keepdims=True)
        for v in range(2):
            z_src[0, :, pl.ds(v * 512 + zp128, 128)] = es[:, v * 128 : v * 128 + 128]
            a_src[0, 0, :, pl.ds(v * 512 + zp128, 128)] = ks[:, v * 128 : v * 128 + 128] * (1.0 / PROTOS)

    got(qg.at[1 - c, zl], gs_rsem.at[0])
    scores(zl)
    for i, step in ((1, 3), (2, 1), (0, 2)):
        zp = lax.rem(zl + step, NZL)
        piece = qg.at[c, zp]
        got(piece, g_rsem.at[i])
        remote(piece, piece, gs_ssem, gs_rsem.at[i + 1], sib).start()
        got(qg.at[1 - c, zp], gs_rsem.at[i + 1])
        scores(zp)

    spec_row = jnp.concatenate([qg[0, i, pl.ds(128, 1)] + qg[1, i, pl.ds(128, 1)] for i in range(4)], axis=1)
    group = lax.broadcasted_iota(jnp.int32, (NGROUP, 512), 0)
    onehot = jnp.where(group == jnp.broadcast_to(spec_row, (NGROUP, 512)).astype(jnp.int32), 1.0, 0.0)

    def a_sum(it, between_1=None, between_2=None):
        for i, to in enumerate(xc_ids):
            remote(a_src.at[it, 0], a_xc.at[it, i], a_ssem.at[it, 0], a_rsem.at[it, 0], to).start()
        if between_1 is not None:
            between_1()
        got(a_xc.at[it], a_rsem.at[it, 0])
        part = a_src[it, 0]
        for i in range(7):
            part = part + a_xc[it, i]
        a_src[it, 1] = part
        for i, to in enumerate(z_ids):
            remote(a_src.at[it, 1], a_z.at[it, i], a_ssem.at[it, 1], a_rsem.at[it, 1], to).start()
        if between_2 is not None:
            between_2()
        got(a_z.at[it], a_rsem.at[it, 1])
        for i in range(7):
            part = part + a_z[it, i]
        return part

    def b_sum(it, between=None):
        for i, to in enumerate(y_ids):
            remote(b_src.at[it], b_y.at[it, i], b_ssem.at[it], b_rsem.at[it], to).start()
        if between is not None:
            between()
        got(b_y.at[it], b_rsem.at[it])
        part = b_src[it]
        for i in range(7):
            part = part + b_y[it, i]
        return part

    def send_counts():
        cnt_src[...] = jnp.broadcast_to(jnp.sum(onehot, axis=1, keepdims=True), (NGROUP, 128))
        for i, to in enumerate(y_ids):
            remote(cnt_src, cnt_y.at[i], cnt_ssem, cnt_rsem, to).start()

    def z_first():
        for i, to in enumerate(xc_ids):
            remote(z_src.at[0], z_xc.at[i], z_ssem.at[0], z_rsem.at[0], to).start()

    def z_second():
        got(z_xc, z_rsem.at[0])
        part = z_src[0]
        for i in range(7):
            part = part + z_xc[i]
        z_src[1] = part
        for i, to in enumerate(z_ids):
            remote(z_src.at[1], z_z.at[i], z_ssem.at[1], z_rsem.at[1], to).start()

    def columns(it, scale):
        for v in range(2):
            out = mm(split3(scale[:, v * 512 : v * 512 + 512]), k_buf[v], NT)
            b_src[it, :, pl.ds(v * 1024, 1024)] = jnp.sum(out, axis=0, keepdims=True)

    def row_sums(it, scale):
        for v in range(2):
            out = mm(split3(scale[:, v * 1024 : v * 1024 + 1024]), k_buf[v])
            a_src[it, 0, :, pl.ds(v * 512, 512)] = jnp.sum(out, axis=0, keepdims=True)

    window_scale = 1.0 / a_sum(0, send_counts)
    columns(0, window_scale)
    proto_scale = 1.0 / (PROTOS * b_sum(0, z_first))
    row_sums(1, proto_scale)
    window_scale = 1.0 / a_sum(1)
    columns(1, window_scale)
    proto_scale = 1.0 / (PROTOS * b_sum(1, z_second))
    row_sums(2, proto_scale)
    window_scale = 1.0 / a_sum(2)
    columns(2, window_scale)
    proto_scale = 1.0 / (PROTOS * b_sum(2))
    row_sums(3, proto_scale)

    def assign():
        for v in range(2):
            for i in range(8):
                p = proto_scale[:, v * 1024 + i * 128 : v * 1024 + i * 128 + 128]
                col = jnp.broadcast_to(p, (128, 128)).T
                for j in range(4):
                    at = (v, pl.ds(i * 128, 128), pl.ds(j * 128, 128))
                    t_buf[at] = k_buf[at].astype(F32) * col

    def cross():
        for v in range(2):

            def block(kb, acc):
                k0 = pl.multiple_of(kb * 32, 32)
                prod = t_buf[1 - v, pl.ds(k0, 32)] * s_buf[v, pl.ds(k0, 32)]
                return acc + jnp.sum(prod.reshape(4, 8, 512), axis=0)

            acc = lax.fori_loop(0, 32, block, jnp.zeros((8, 512), F32))
            x_rows[v] = jnp.sum(acc, axis=0, keepdims=True)

    last = 1.0 / a_sum(3, assign, cross)

    got(z_z, z_rsem.at[1])
    totals = z_src[1]
    for i in range(7):
        totals = totals + z_z[i]
    got(cnt_y, cnt_rsem)
    counts = cnt_src[...]
    for i in range(7):
        counts = counts + cnt_y[i]
    seen = jnp.sum(onehot * jnp.concatenate([counts] * 4, axis=1), axis=0, keepdims=True)
    weight = WINDOWS / (NGROUP * seen)
    last_v = [last[:, 0:512], last[:, 512:1024]]
    tot_v = [totals[:, 0:512], totals[:, 512:1024]]
    a_v = [5.0 * weight / tot_v[v] for v in range(2)]
    b_v = [5.0 * weight * last_v[1 - v] for v in range(2)]
    terms = jnp.zeros((1, 512), F32)
    for v in range(2):
        terms = terms + 0.5 * weight * (jnp.log(tot_v[v]) / 64.0 - 10.0 * last_v[1 - v] * x_rows[v])
    terms = terms[:, 0:128] + terms[:, 128:256] + terms[:, 256:384] + terms[:, 384:512]
    me_xc = x * NC + c
    l_xc[me_xc] = terms
    for to in xc_ids:
        remote(l_xc.at[me_xc], l_xc.at[me_xc], l_ssem.at[0], l_rsem.at[0], to).start()

    def add_slots(ref):
        out = ref[0]
        for i in range(1, 8):
            out = out + ref[i]
        return out

    for i, yy in enumerate(y_of + [y]):
        k0 = pl.multiple_of(yy * 128, 128)
        part = jnp.zeros((128, FEAT), F32)
        for v in range(2):
            at = (pl.ds(k0, 128), slice(None))
            g = (e_buf[(v,) + at] * a_v[v] - t_buf[(1 - v,) + at] * b_v[v]).astype(BF16)
            g_buf[(v,) + at] = g
            part = part + mm(g, q16[v])
        kg_src[i] = part
        if i < 7:
            remote(kg_src.at[i], kg_y.at[i], kg_ssem, kg_rsem, y_ids[i]).start()

    c_src[...] = mm(keys_t[...], g_buf[1 - c])
    remote(c_src, c_rcv, f_ssem.at[0], f_rsem.at[0], sib).start()
    own = mm(keys_t[...], g_buf[c])
    got(c_rcv, f_rsem.at[0])
    x_src[...] = own + c_rcv[...]
    for i, xx in enumerate(x_of):
        remote(x_src.at[pl.ds(pl.multiple_of(xx * 32, 32), 32)], x_rcv.at[i], f_ssem.at[1], f_rsem.at[1], x_ids[i]).start()
    got(x_rcv, f_rsem.at[1])
    part = x_src[pl.ds(pl.multiple_of(x * 32, 32), 32)] + x_rcv[0] + x_rcv[1] + x_rcv[2]
    for i in range(4):
        w_src[i] = part[:, i * 128 : i * 128 + 128]
    others = [l for l in range(8)]
    got(l_xc.at[pl.ds(0, 7)], l_rsem.at[0])
    l_z[z] = add_slots(l_xc)
    for i, to in enumerate(z_ids):
        remote(l_z.at[z], l_z.at[z], l_ssem.at[1], l_rsem.at[1], to).start()
        remote(w_src.at[lax.rem(z_of[i], NZL)], w_rcv.at[i], f_ssem.at[2], f_rsem.at[2], to).start()
    got(w_rcv, f_rsem.at[2])
    part = w_src[zl]
    for i in range(7):
        part = part + w_rcv[i]
    mine = fin.at[c, pl.ds(pl.multiple_of(x * 32, 32), 32)]
    fin[c, pl.ds(pl.multiple_of(x * 32, 32), 32)] = part
    for to in xc_ids:
        remote(mine, mine, f_ssem.at[3], f_rsem.at[3], to).start()
    got(l_z.at[pl.ds(0, 7)], l_rsem.at[1])
    l_y[y] = add_slots(l_z)
    for to in y_ids:
        remote(l_y.at[y], l_y.at[y], l_ssem.at[2], l_rsem.at[2], to).start()

    got(kg_y, kg_rsem)
    part = kg_src[7]
    for i in range(7):
        part = part + kg_y[i]
    pgrad_ref[...] = unit_back(kraw[y].astype(F32), part)

    got(w_rcv, f_rsem.at[3])
    for v in range(2):
        qt[v] = fin[v].T
    for v in range(2):
        grad = qt[v, pl.ds(pl.multiple_of(c * 64, 64), 64)]
        view_ref[v] = unit_back(pooled[pl.ds(v * 64, 64)], grad)

    got(l_y.at[pl.ds(0, 7)], l_rsem.at[2])
    loss_ref[...] = jnp.sum(add_slots(l_y), axis=1, keepdims=True) * (1.0 / WINDOWS)

    sent(qg.at[0, pl.ds(0, 3)], g_ssem)
    sent(qg.at[0], gs_ssem)
    for it in range(4):
        sent(a_xc.at[it], a_ssem.at[it, 0])
        sent(a_z.at[it], a_ssem.at[it, 1])
    for it in range(3):
        sent(b_y.at[it], b_ssem.at[it])
    sent(z_xc, z_ssem.at[0])
    sent(z_z, z_ssem.at[1])
    sent(cnt_y, cnt_ssem)
    sent(kg_y, kg_ssem)
    sent(c_rcv, f_ssem.at[0])
    sent(x_rcv, f_ssem.at[1])
    sent(w_rcv, f_ssem.at[2])
    sent(w_rcv, f_ssem.at[3])
    for i in range(3):
        sent(l_xc.at[pl.ds(0, 7)], l_ssem.at[i])


def on_device(tokens, offsets, species, prototypes):
    vmem = pltpu.VMEM
    dma = pltpu.SemaphoreType.DMA
    anywhere = pl.BlockSpec(memory_space=pl.ANY)
    inside = pl.BlockSpec(memory_space=pltpu.VMEM)
    scratch = [
        vmem((64 * SEQ, FEAT), BF16),
        vmem((8, 128, FEAT), BF16),
        vmem((1024, FEAT), BF16),
        vmem((FEAT, 1024), BF16),
        vmem((128, FEAT), F32),
        vmem((2, 4, 136, FEAT), F32),
        vmem((2, 512, FEAT), BF16),
        vmem((2, 1024, 512), F32),
        vmem((2, 1024, 512), F32),
        vmem((2, 1024, 512), BF16),
        vmem((2, 1024, 512), F32),
        vmem((2, 1024, 512), BF16),
        vmem((4, 2, 1, 1024), F32),
        vmem((4, 7, 1, 1024), F32),
        vmem((4, 7, 1, 1024), F32),
        vmem((3, 1, 2048), F32),
        vmem((3, 7, 1, 2048), F32),
        vmem((2, 1, 1024), F32),
        vmem((7, 1, 1024), F32),
        vmem((7, 1, 1024), F32),
        vmem((NGROUP, 128), F32),
        vmem((7, NGROUP, 128), F32),
        vmem((8, 128, FEAT), F32),
        vmem((7, 128, FEAT), F32),
        vmem((FEAT, 512), F32),
        vmem((FEAT, 512), F32),
        vmem((FEAT, 512), F32),
        vmem((3, 32, 512), F32),
        vmem((4, 32, 128), F32),
        vmem((7, 32, 128), F32),
        vmem((2, FEAT, 128), F32),
        vmem((8, 1, 128), F32),
        vmem((8, 1, 128), F32),
        vmem((8, 1, 128), F32),
        vmem((2, 1, 512), F32),
        vmem((2, 128, FEAT), F32),
        dma((2,)),
        dma, dma((3,)), dma, dma((4,)),
        dma((4, 2)), dma((4, 2)), dma((3,)), dma((3,)), dma((2,)), dma((2,)), dma, dma,
        dma, dma, dma((4,)), dma((4,)), dma((3,)), dma((3,)),
    ]
    view_grads, proto_grads, loss = pl.pallas_call(
        kernel,
        out_shape=(
            jax.ShapeDtypeStruct((2, 64, FEAT), F32),
            jax.ShapeDtypeStruct((128, FEAT), F32),
            jax.ShapeDtypeStruct((1, 1), F32),
        ),
        in_specs=[anywhere, inside, inside, anywhere],
        out_specs=(inside, inside, inside),
        scratch_shapes=scratch,
        compiler_params=pltpu.CompilerParams(
            collective_id=0, has_side_effects=True, vmem_limit_bytes=56 * 2**20
        ),
        name="swav_step",
    )(
        tokens.reshape(64 * SEQ, FEAT),
        offsets,
        species.reshape(1, 64),
        prototypes.reshape(8, 8, 128, FEAT),
    )
    return view_grads, proto_grads, loss.reshape(())


def solution(mesh):
    return jax.shard_map(
        on_device,
        mesh=mesh,
        in_specs=(P("dp", None, None), P(None, "dp"), P("dp"), P("proto", None)),
        out_specs=(P(None, "dp", None), P(("proto", "dp"), None), P()),
        check_vma=False,
    )
```

time: 1960 us -> 103 us (0.05)
  waiting for transfers between devices: 1520 us -> 0 us
  blocking collectives: 381 us -> 0 us
  Pallas kernels: 0 us -> 97.7 us
  other arithmetic: 24 us -> 0 us
    psum x4 -> x0, waiting for transfers between devices: 1240 us -> none  [the longest x3 1240 us: on_device(): columns = lax.psum(local_sums, 'dp')]
    psum x7 -> x0, blocking collectives: 381 us -> none  [the longest x1 141 us: on_device(): counts = lax.psum(local_counts, 'dp')]
    reduce_scatter x1 -> x0, waiting for transfers between devices: 281 us -> none  [on_device(): lax.psum_scatter(key_term_full, 'dp', scatter_dimension=0, tiled=True)]
    pallas_call x0 -> x1, Pallas kernels: none -> 97.7 us  [on_device(): pl.pallas_call(kernel, out_shape=(jax.ShapeDtypeStruct((2, 64, FEAT), F32...]
  transfers between devices with their start and end apart: 5 -> 0, of which waited for: 4 -> 0; matrix products, arithmetic and copies ran while one was open for 0% -> 0% of each run, Pallas kernels for 0% -> 0%
where the time goes in v1:
time: 103 us
  Pallas kernels  97.7 us (95%)
  local copies, waits for them, and re-layouts  2.95 us (3%)
  between operations  2.45 us (2%)
    pallas_call x1, Pallas kernels, on_device(): pl.pallas_call(kernel, out_shape=(jax.ShapeDtypeStruct((2, 64, FEAT), F32...  97.7 us
    unnamed x2, local copies, waits for them, and re-layouts  2.95 us

profile of v1, /device:TPU:1, one launch (start us, length us, event | category | flops | bytes accessed | tf_op | source)
XLA Modules:
  0.0 103.1 jit_solution(811021113375879095)
XLA Ops:
  0.6 97.7 %swav_step.1 = (f32[2,64,128]{2,1,0:T(8,128)}, f32[128,128]{1,0:T(8,128)}, f32[1,1]{1,0:T(1,128)}) custom-call(bf16[2048,128]{1,0:T(8,128)(2,1)} %bitcast.5, s32[2,64]{1,0:T(2,128)} %off_ref.1, s32[1,64]{1,0:T(1,128)} %bitcast.6, bf16[8,8,128,128]{3,2,1,0:T(8,128)(2,1)} %bitcast.4), custom_call_target="tpu_custom_call" | custom-call | tf_op jit(solution)/shard_map/swav_step/pallas_call | solution.py:433
  98.4 1.5 %copy.10 = f32[2,64,128]{2,1,0:T(8,128)} copy(f32[2,64,128]{2,1,0:T(8,128)} %get-tuple-element.12) | data formatting | bytes 131072
  99.8 1.5 %copy.11 = f32[128,128]{1,0:T(8,128)} copy(f32[128,128]{1,0:T(8,128)} %get-tuple-element.13) | data formatting | bytes 131072

commit v2 on v1

--- a/solution.py
+++ b/solution.py
@@ -22,6 +22,13 @@
 RING8 = (4, 3, 5, 2, 6, 1, 7)
 XC = ((2, 0), (2, 1), (1, 0), (3, 0), (1, 1), (3, 1), (0, 1))
 RING4 = (2, 1, 3)
+PLANE = tuple(
+    sorted(
+        ((dx, dz) for dx in range(NX) for dz in range(NZ) if dx or dz),
+        key=lambda o: -(min(o[0], NX - o[0]) + min(o[1], NZ - o[1])),
+    )
+)
+NP = len(PLANE)
 NT = (((1,), (1,)), ((), ()))
 NN = (((1,), (0,)), ((), ()))
 
@@ -55,13 +62,13 @@
 def kernel(
     tok_ref, off_ref, spec_ref, proto_ref,
     view_ref, pgrad_ref, loss_ref,
-    tok, kraw, keys, keys_t, pooled, qg, q16, s_buf, e_buf, k_buf, t_buf, g_buf,
-    a_src, a_xc, a_z, b_src, b_y, z_src, z_xc, z_z, cnt_src, cnt_y,
-    kg_src, kg_y, c_src, c_rcv, x_src, x_rcv, w_src, w_rcv, fin, l_xc, l_z, l_y,
-    x_rows, qt,
+    tok, kraw, keys, keys_t, pooled, qg, q16, s_buf, e_buf, k_buf, t_buf, two,
+    a_src, a_c, a_pl, b_src, b_y, z_src, z_c, z_pl, cnt_src, cnt_y,
+    kg_src, kg_half, kg_fwd, kg_y, c_src, c_rcv, x_src, x_rcv, w_src, w_rcv, fin, l_xc, l_z, l_y,
+    x_rows, p_row, ab_rows, qt,
     load_sem, g_ssem, g_rsem, gs_ssem, gs_rsem,
     a_ssem, a_rsem, b_ssem, b_rsem, z_ssem, z_rsem, cnt_ssem, cnt_rsem,
-    kg_ssem, kg_rsem, f_ssem, f_rsem, l_ssem, l_rsem,
+    kg_ssem, kg_rsem, f_ssem, f_rsem, fin_ssem, fin_rsem, l_ssem, l_rsem,
 ):
     dp = lax.axis_index("dp")
     pr = lax.axis_index("proto")
@@ -80,6 +87,8 @@
     x_of = [lax.rem(x + j, NX) for j in RING4]
     x_ids = [dev(x=k) for k in x_of]
     sib = dev(c=1 - c)
+    plane_ids = [dev(x=lax.rem(x + dx, NX), z=lax.rem(z + dz, NZ)) for dx, dz in PLANE]
+    cross_ids = [xc_ids[i] for i in range(7) if XC[i][0] and XC[i][1]]
 
     def remote(src, dst, ssem, rsem, to):
         return pltpu.make_async_remote_copy(
@@ -97,7 +106,7 @@
     load_key = pltpu.make_async_copy(proto_ref.at[:, zl * NC + c], kraw, load_sem.at[1])
     load_tok.start()
     load_key.start()
-    for to in xc_ids + z_ids + y_ids:
+    for to in [sib] + plane_ids + cross_ids + y_ids:
         pl.semaphore_signal(barrier, inc=1, device_id=to, device_id_type=MESH)
 
     off = off_ref[...].astype(F32)
@@ -126,7 +135,7 @@
     half = lax.broadcasted_iota(jnp.int32, (8, 128), 1) // 64
     qg[c, zl, pl.ds(128, 8)] = jnp.where(half == c, jnp.broadcast_to(both, (8, 128)), 0.0)
 
-    pl.semaphore_wait(barrier, 21)
+    pl.semaphore_wait(barrier, 11 + NP)
     step2 = 2 + 4 * c
     mine = qg.at[c, zl]
     for i, to in enumerate((dev(z=lax.rem(z + step2, NZ)), dev(z=lax.rem(z + 1, NZ)), dev(z=lax.rem(z + 7, NZ)))):
@@ -138,7 +147,9 @@
         raw = kraw[i].astype(F32)
         unit = raw * unit_scale(raw) / math.sqrt(FEAT)
         keys[pl.ds(i * 128, 128)] = unit.astype(BF16)
-        keys_t[:, pl.ds(i * 128, 128)] = unit.astype(BF16).astype(F32).T.astype(BF16)
+        turned = unit.astype(BF16).astype(F32).T.astype(BF16)
+        keys_t[:, pl.ds(i * 128, 128)] = turned
+        keys_t[:, pl.ds(1024 + i * 128, 128)] = turned
 
     def scores(zp):
         zp128 = pl.multiple_of(zp * 128, 128)
@@ -185,22 +196,19 @@
     onehot = jnp.where(group == jnp.broadcast_to(spec_row, (NGROUP, 512)).astype(jnp.int32), 1.0, 0.0)
 
     def a_sum(it, between_1=None, between_2=None):
-        for i, to in enumerate(xc_ids):
-            remote(a_src.at[it, 0], a_xc.at[it, i], a_ssem.at[it, 0], a_rsem.at[it, 0], to).start()
+        remote(a_src.at[it, 0], a_c.at[it], a_ssem.at[it, 0], a_rsem.at[it, 0], sib).start()
         if between_1 is not None:
             between_1()
-        got(a_xc.at[it], a_rsem.at[it, 0])
-        part = a_src[it, 0]
-        for i in range(7):
-            part = part + a_xc[it, i]
+        got(a_c.at[it], a_rsem.at[it, 0])
+        part = a_src[it, 0] + a_c[it]
         a_src[it, 1] = part
-        for i, to in enumerate(z_ids):
-            remote(a_src.at[it, 1], a_z.at[it, i], a_ssem.at[it, 1], a_rsem.at[it, 1], to).start()
+        for i, to in enumerate(plane_ids):
+            remote(a_src.at[it, 1], a_pl.at[it, i], a_ssem.at[it, 1], a_rsem.at[it, 1], to).start()
         if between_2 is not None:
             between_2()
-        got(a_z.at[it], a_rsem.at[it, 1])
-        for i in range(7):
-            part = part + a_z[it, i]
+        got(a_pl.at[it], a_rsem.at[it, 1])
+        for i in range(NP):
+            part = part + a_pl[it, i]
         return part
 
     def b_sum(it, between=None):
@@ -220,17 +228,68 @@
             remote(cnt_src, cnt_y.at[i], cnt_ssem, cnt_rsem, to).start()
 
     def z_first():
-        for i, to in enumerate(xc_ids):
-            remote(z_src.at[0], z_xc.at[i], z_ssem.at[0], z_rsem.at[0], to).start()
+        remote(z_src.at[0], z_c, z_ssem.at[0], z_rsem.at[0], sib).start()
 
     def z_second():
-        got(z_xc, z_rsem.at[0])
-        part = z_src[0]
+        got(z_c, z_rsem.at[0])
+        z_src[1] = z_src[0] + z_c[...]
+        for i, to in enumerate(plane_ids):
+            remote(z_src.at[1], z_pl.at[i], z_ssem.at[1], z_rsem.at[1], to).start()
+
+    def halves(value, k0, width):
+        hi = value.astype(BF16)
+        two[pl.ds(k0, width)] = hi
+        two[pl.ds(1024 + k0, width)] = (value - hi.astype(F32)).astype(BF16)
+
+    def split_e(v):
+        def block(kb, carry):
+            k0 = pl.multiple_of(kb * 32, 32)
+            halves(e_buf[v, pl.ds(k0, 32)], k0, 32)
+            return carry
+
+        lax.fori_loop(0, 32, block, 0)
+
+    def split_t(v):
+        for i in range(8):
+            p = p_row[:, pl.ds(pl.multiple_of(v * 1024 + i * 128, 128), 128)]
+            col = jnp.broadcast_to(p, (128, 128)).T
+            t = k_buf[v, pl.ds(i * 128, 128)].astype(F32) * jnp.concatenate([col] * 4, axis=1)
+            t_buf[v, pl.ds(i * 128, 128)] = t
+            halves(t, i * 128, 128)
+
+    def q_core(step):
+        prepare = (split_e, split_t)[step]
+        theirs = 1 - c if step == 0 else c
+        prepare(theirs)
+        c_src[step] = mm(keys_t[...], two[...])
+        remote(c_src.at[step], c_rcv.at[step], f_ssem.at[step, 0], f_rsem.at[step, 0], sib).start()
+        prepare(1 - theirs)
+        x_src[step] = mm(keys_t[...], two[...])
+
+    def q_x(step):
+        got(c_rcv.at[step], f_rsem.at[step, 0])
+        x_src[step] = x_src[step] + c_rcv[step]
+        for i, xx in enumerate(x_of):
+            piece = x_src.at[step, pl.ds(pl.multiple_of(xx * 32, 32), 32)]
+            remote(piece, x_rcv.at[step, i], f_ssem.at[step, 1], f_rsem.at[step, 1], x_ids[i]).start()
+
+    def q_z(step):
+        got(x_rcv.at[step], f_rsem.at[step, 1])
+        part = x_src[step, pl.ds(pl.multiple_of(x * 32, 32), 32)]
+        for i in range(3):
+            part = part + x_rcv[step, i]
+        for i in range(4):
+            w_src[step, i] = part[:, i * 128 : i * 128 + 128]
+        for i, to in enumerate(z_ids):
+            piece = w_src.at[step, lax.rem(z_of[i], NZL)]
+            remote(piece, w_rcv.at[step, i], f_ssem.at[step, 2], f_rsem.at[step, 2], to).start()
+
+    def q_end(step):
+        got(w_rcv.at[step], f_rsem.at[step, 2])
+        part = w_src[step, zl]
         for i in range(7):
-            part = part + z_xc[i]
-        z_src[1] = part
-        for i, to in enumerate(z_ids):
-            remote(z_src.at[1], z_z.at[i], z_ssem.at[1], z_rsem.at[1], to).start()
+            part = part + w_rcv[step, i]
+        return part
 
     def columns(it, scale):
         for v in range(2):
@@ -242,27 +301,31 @@
             out = mm(split3(scale[:, v * 1024 : v * 1024 + 1024]), k_buf[v])
             a_src[it, 0, :, pl.ds(v * 512, 512)] = jnp.sum(out, axis=0, keepdims=True)
 
-    window_scale = 1.0 / a_sum(0, send_counts)
+    def beside_a0():
+        send_counts()
+        q_core(0)
+
+    def beside_b0():
+        z_first()
+        q_x(0)
+
+    def beside_b1():
+        z_second()
+        q_z(0)
+
+    window_scale = 1.0 / a_sum(0, None, beside_a0)
     columns(0, window_scale)
-    proto_scale = 1.0 / (PROTOS * b_sum(0, z_first))
+    proto_scale = 1.0 / (PROTOS * b_sum(0, beside_b0))
     row_sums(1, proto_scale)
     window_scale = 1.0 / a_sum(1)
     columns(1, window_scale)
-    proto_scale = 1.0 / (PROTOS * b_sum(1, z_second))
+    proto_scale = 1.0 / (PROTOS * b_sum(1, beside_b1))
     row_sums(2, proto_scale)
     window_scale = 1.0 / a_sum(2)
     columns(2, window_scale)
     proto_scale = 1.0 / (PROTOS * b_sum(2))
     row_sums(3, proto_scale)
-
-    def assign():
-        for v in range(2):
-            for i in range(8):
-                p = proto_scale[:, v * 1024 + i * 128 : v * 1024 + i * 128 + 128]
-                col = jnp.broadcast_to(p, (128, 128)).T
-                for j in range(4):
-                    at = (v, pl.ds(i * 128, 128), pl.ds(j * 128, 128))
-                    t_buf[at] = k_buf[at].astype(F32) * col
+    p_row[...] = proto_scale
 
     def cross():
         for v in range(2):
@@ -275,12 +338,17 @@
             acc = lax.fori_loop(0, 32, block, jnp.zeros((8, 512), F32))
             x_rows[v] = jnp.sum(acc, axis=0, keepdims=True)
 
-    last = 1.0 / a_sum(3, assign, cross)
-
-    got(z_z, z_rsem.at[1])
+    def beside_a3():
+        q_core(1)
+        q_x(1)
+        cross()
+
+    last = 1.0 / a_sum(3, None, beside_a3)
+
+    got(z_pl, z_rsem.at[1])
     totals = z_src[1]
-    for i in range(7):
-        totals = totals + z_z[i]
+    for i in range(NP):
+        totals = totals + z_pl[i]
     got(cnt_y, cnt_rsem)
     counts = cnt_src[...]
     for i in range(7):
@@ -291,6 +359,9 @@
     tot_v = [totals[:, 0:512], totals[:, 512:1024]]
     a_v = [5.0 * weight / tot_v[v] for v in range(2)]
     b_v = [5.0 * weight * last_v[1 - v] for v in range(2)]
+    for v in range(2):
+        ab_rows[0, v] = a_v[v]
+        ab_rows[1, v] = b_v[v]
     terms = jnp.zeros((1, 512), F32)
     for v in range(2):
         terms = terms + 0.5 * weight * (jnp.log(tot_v[v]) / 64.0 - 10.0 * last_v[1 - v] * x_rows[v])
@@ -306,55 +377,67 @@
             out = out + ref[i]
         return out
 
-    for i, yy in enumerate(y_of + [y]):
+    def key_part(slot, yy):
         k0 = pl.multiple_of(yy * 128, 128)
         part = jnp.zeros((128, FEAT), F32)
         for v in range(2):
             at = (pl.ds(k0, 128), slice(None))
             g = (e_buf[(v,) + at] * a_v[v] - t_buf[(1 - v,) + at] * b_v[v]).astype(BF16)
-            g_buf[(v,) + at] = g
             part = part + mm(g, q16[v])
-        kg_src[i] = part
-        if i < 7:
-            remote(kg_src.at[i], kg_y.at[i], kg_ssem, kg_rsem, y_ids[i]).start()
-
-    c_src[...] = mm(keys_t[...], g_buf[1 - c])
-    remote(c_src, c_rcv, f_ssem.at[0], f_rsem.at[0], sib).start()
-    own = mm(keys_t[...], g_buf[c])
-    got(c_rcv, f_rsem.at[0])
-    x_src[...] = own + c_rcv[...]
-    for i, xx in enumerate(x_of):
-        remote(x_src.at[pl.ds(pl.multiple_of(xx * 32, 32), 32)], x_rcv.at[i], f_ssem.at[1], f_rsem.at[1], x_ids[i]).start()
-    got(x_rcv, f_rsem.at[1])
-    part = x_src[pl.ds(pl.multiple_of(x * 32, 32), 32)] + x_rcv[0] + x_rcv[1] + x_rcv[2]
-    for i in range(4):
-        w_src[i] = part[:, i * 128 : i * 128 + 128]
-    others = [l for l in range(8)]
+        kg_src[slot] = part
+
+    ahead = lambda j: lax.rem(y + j, NY)
+    up1, up2, down1, down2 = (dev(y=ahead(j)) for j in (1, 2, 7, 6))
+    key_part(4, ahead(4))
+    remote(kg_src.at[4, pl.ds(0, 64)], kg_half.at[0], kg_ssem.at[0], kg_rsem.at[0], up2).start()
+    remote(kg_src.at[4, pl.ds(64, 64)], kg_half.at[1], kg_ssem.at[1], kg_rsem.at[1], down2).start()
+    key_part(3, ahead(3))
+    remote(kg_src.at[3], kg_fwd.at[0], kg_ssem.at[2], kg_rsem.at[2], up1).start()
+    key_part(5, ahead(5))
+    remote(kg_src.at[5], kg_fwd.at[1], kg_ssem.at[3], kg_rsem.at[3], down1).start()
+    key_part(2, ahead(2))
+    key_part(6, ahead(6))
+    key_part(1, ahead(1))
+    remote(kg_src.at[1], kg_y.at[0], kg_ssem.at[4], kg_rsem.at[4], up1).start()
+    key_part(7, ahead(7))
+    remote(kg_src.at[7], kg_y.at[1], kg_ssem.at[5], kg_rsem.at[5], down1).start()
+    key_part(0, y)
+
+    q_z(1)
+    got(kg_fwd.at[0], kg_rsem.at[2])
+    got(kg_half.at[0], kg_rsem.at[0])
+    kg_src[2, pl.ds(0, 64)] = kg_src[2, pl.ds(0, 64)] + kg_fwd[0, pl.ds(0, 64)] + kg_half[0]
+    kg_src[2, pl.ds(64, 64)] = kg_src[2, pl.ds(64, 64)] + kg_fwd[0, pl.ds(64, 64)]
+    remote(kg_src.at[2], kg_y.at[2], kg_ssem.at[6], kg_rsem.at[6], up2).start()
+    got(kg_fwd.at[1], kg_rsem.at[3])
+    got(kg_half.at[1], kg_rsem.at[1])
+    kg_src[6, pl.ds(0, 64)] = kg_src[6, pl.ds(0, 64)] + kg_fwd[1, pl.ds(0, 64)]
+    kg_src[6, pl.ds(64, 64)] = kg_src[6, pl.ds(64, 64)] + kg_fwd[1, pl.ds(64, 64)] + kg_half[1]
+    remote(kg_src.at[6], kg_y.at[3], kg_ssem.at[7], kg_rsem.at[7], down2).start()
+
     got(l_xc.at[pl.ds(0, 7)], l_rsem.at[0])
     l_z[z] = add_slots(l_xc)
-    for i, to in enumerate(z_ids):
+    for to in z_ids:
         remote(l_z.at[z], l_z.at[z], l_ssem.at[1], l_rsem.at[1], to).start()
-        remote(w_src.at[lax.rem(z_of[i], NZL)], w_rcv.at[i], f_ssem.at[2], f_rsem.at[2], to).start()
-    got(w_rcv, f_rsem.at[2])
-    part = w_src[zl]
-    for i in range(7):
-        part = part + w_rcv[i]
+
+    at = pl.ds(pl.multiple_of(zl * 128, 128), 128)
+    part = ab_rows[0, c, :, at] * q_end(0) - ab_rows[1, c, :, at] * q_end(1)
     mine = fin.at[c, pl.ds(pl.multiple_of(x * 32, 32), 32)]
     fin[c, pl.ds(pl.multiple_of(x * 32, 32), 32)] = part
     for to in xc_ids:
-        remote(mine, mine, f_ssem.at[3], f_rsem.at[3], to).start()
+        remote(mine, mine, fin_ssem, fin_rsem, to).start()
     got(l_z.at[pl.ds(0, 7)], l_rsem.at[1])
     l_y[y] = add_slots(l_z)
     for to in y_ids:
         remote(l_y.at[y], l_y.at[y], l_ssem.at[2], l_rsem.at[2], to).start()
 
-    got(kg_y, kg_rsem)
-    part = kg_src[7]
-    for i in range(7):
+    part = kg_src[0]
+    for i, k in ((0, 4), (1, 5), (2, 6), (3, 7)):
+        got(kg_y.at[i], kg_rsem.at[k])
         part = part + kg_y[i]
     pgrad_ref[...] = unit_back(kraw[y].astype(F32), part)
 
-    got(w_rcv, f_rsem.at[3])
+    got(w_rcv.at[0], fin_rsem)
     for v in range(2):
         qt[v] = fin[v].T
     for v in range(2):
@@ -367,18 +450,22 @@
     sent(qg.at[0, pl.ds(0, 3)], g_ssem)
     sent(qg.at[0], gs_ssem)
     for it in range(4):
-        sent(a_xc.at[it], a_ssem.at[it, 0])
-        sent(a_z.at[it], a_ssem.at[it, 1])
+        sent(a_c.at[it], a_ssem.at[it, 0])
+        sent(a_pl.at[it], a_ssem.at[it, 1])
     for it in range(3):
         sent(b_y.at[it], b_ssem.at[it])
-    sent(z_xc, z_ssem.at[0])
-    sent(z_z, z_ssem.at[1])
+    sent(z_c, z_ssem.at[0])
+    sent(z_pl, z_ssem.at[1])
     sent(cnt_y, cnt_ssem)
-    sent(kg_y, kg_ssem)
-    sent(c_rcv, f_ssem.at[0])
-    sent(x_rcv, f_ssem.at[1])
-    sent(w_rcv, f_ssem.at[2])
-    sent(w_rcv, f_ssem.at[3])
+    for i in range(2):
+        sent(kg_half.at[i], kg_ssem.at[i])
+        sent(kg_fwd.at[i], kg_ssem.at[2 + i])
+        sent(kg_y.at[i], kg_ssem.at[4 + i])
+        sent(kg_y.at[2 + i], kg_ssem.at[6 + i])
+        sent(c_rcv.at[i], f_ssem.at[i, 0])
+        sent(x_rcv.at[i], f_ssem.at[i, 1])
+        sent(w_rcv.at[i], f_ssem.at[i, 2])
+    sent(w_rcv.at[0], fin_ssem)
     for i in range(3):
         sent(l_xc.at[pl.ds(0, 7)], l_ssem.at[i])
 
@@ -392,7 +479,7 @@
         vmem((64 * SEQ, FEAT), BF16),
         vmem((8, 128, FEAT), BF16),
         vmem((1024, FEAT), BF16),
-        vmem((FEAT, 1024), BF16),
+        vmem((FEAT, 2048), BF16),
         vmem((128, FEAT), F32),
         vmem((2, 4, 136, FEAT), F32),
         vmem((2, 512, FEAT), BF16),
@@ -400,35 +487,39 @@
         vmem((2, 1024, 512), F32),
         vmem((2, 1024, 512), BF16),
         vmem((2, 1024, 512), F32),
-        vmem((2, 1024, 512), BF16),
+        vmem((2048, 512), BF16),
         vmem((4, 2, 1, 1024), F32),
-        vmem((4, 7, 1, 1024), F32),
-        vmem((4, 7, 1, 1024), F32),
+        vmem((4, 1, 1024), F32),
+        vmem((4, NP, 1, 1024), F32),
         vmem((3, 1, 2048), F32),
         vmem((3, 7, 1, 2048), F32),
         vmem((2, 1, 1024), F32),
-        vmem((7, 1, 1024), F32),
-        vmem((7, 1, 1024), F32),
+        vmem((1, 1024), F32),
+        vmem((NP, 1, 1024), F32),
         vmem((NGROUP, 128), F32),
         vmem((7, NGROUP, 128), F32),
         vmem((8, 128, FEAT), F32),
-        vmem((7, 128, FEAT), F32),
-        vmem((FEAT, 512), F32),
-        vmem((FEAT, 512), F32),
-        vmem((FEAT, 512), F32),
-        vmem((3, 32, 512), F32),
-        vmem((4, 32, 128), F32),
-        vmem((7, 32, 128), F32),
+        vmem((2, 64, FEAT), F32),
+        vmem((2, 128, FEAT), F32),
+        vmem((4, 128, FEAT), F32),
+        vmem((2, FEAT, 512), F32),
+        vmem((2, FEAT, 512), F32),
+        vmem((2, FEAT, 512), F32),
+        vmem((2, 3, 32, 512), F32),
+        vmem((2, 4, 32, 128), F32),
+        vmem((2, 7, 32, 128), F32),
         vmem((2, FEAT, 128), F32),
         vmem((8, 1, 128), F32),
         vmem((8, 1, 128), F32),
         vmem((8, 1, 128), F32),
         vmem((2, 1, 512), F32),
+        vmem((1, 2048), F32),
+        vmem((2, 2, 1, 512), F32),
         vmem((2, 128, FEAT), F32),
         dma((2,)),
         dma, dma((3,)), dma, dma((4,)),
         dma((4, 2)), dma((4, 2)), dma((3,)), dma((3,)), dma((2,)), dma((2,)), dma, dma,
-        dma, dma, dma((4,)), dma((4,)), dma((3,)), dma((3,)),
+        dma((8,)), dma((8,)), dma((2, 3)), dma((2, 3)), dma, dma, dma((3,)), dma((3,)),
     ]
     view_grads, proto_grads, loss = pl.pallas_call(
         kernel,

time: 103 us -> 95.7 us (0.929)
  Pallas kernels: 97.7 us -> 90 us
    pallas_call x1, Pallas kernels: 97.7 us -> 90 us  [on_device(): pl.pallas_call(kernel, out_shape=(jax.ShapeDtypeStruct((2, 64, FEAT), F32...]
where the time goes in v2:
time: 95.7 us; the launch traced here: 95.4 us
  Pallas kernels  90 us (94%)
  local copies, waits for them, and re-layouts  2.95 us (3%)
  between operations  2.45 us (3%)
    pallas_call x1, Pallas kernels, on_device(): pl.pallas_call(kernel, out_shape=(jax.ShapeDtypeStruct((2, 64, FEAT), F32...  90 us
    unnamed x2, local copies, waits for them, and re-layouts  2.95 us

profile of v2, /device:TPU:1, one launch (start us, length us, event | category | flops | bytes accessed | tf_op | source)
XLA Modules:
  0.0 95.4 jit_solution(18308042272000172933)
XLA Ops:
  0.6 90.0 %swav_step.1 = (f32[2,64,128]{2,1,0:T(8,128)}, f32[128,128]{1,0:T(8,128)}, f32[1,1]{1,0:T(1,128)}) custom-call(bf16[2048,128]{1,0:T(8,128)(2,1)} %bitcast.5, s32[2,64]{1,0:T(2,128)} %off_ref.1, s32[1,64]{1,0:T(1,128)} %bitcast.6, bf16[8,8,128,128]{3,2,1,0:T(8,128)(2,1)} %bitcast.4), custom_call_target="tpu_custom_call" | custom-call | tf_op jit(solution)/shard_map/swav_step/pallas_call | solution.py:524
  90.7 1.5 %copy.10 = f32[2,64,128]{2,1,0:T(8,128)} copy(f32[2,64,128]{2,1,0:T(8,128)} %get-tuple-element.12) | data formatting | bytes 131072
  92.1 1.5 %copy.11 = f32[128,128]{1,0:T(8,128)} copy(f32[128,128]{1,0:T(8,128)} %get-tuple-element.13) | data formatting | bytes 131072

commit v3 on v2

--- a/solution.py
+++ b/solution.py
@@ -62,12 +62,12 @@
 def kernel(
     tok_ref, off_ref, spec_ref, proto_ref,
     view_ref, pgrad_ref, loss_ref,
-    tok, kraw, keys, keys_t, pooled, qg, q16, s_buf, e_buf, k_buf, t_buf, two,
-    a_src, a_c, a_pl, b_src, b_y, z_src, z_c, z_pl, cnt_src, cnt_y,
+    tok, mask, kraw, kunit, keys, keys_t, pooled, qg, q16, s_buf, e_buf, k_buf, t_buf, two,
+    a_src, a_c, a_pl, b_src, b_y, r_src, r_px, r_mem, cnt_src, cnt_y,
     kg_src, kg_half, kg_fwd, kg_y, c_src, c_rcv, x_src, x_rcv, w_src, w_rcv, fin, l_xc, l_z, l_y,
     x_rows, p_row, ab_rows, qt,
     load_sem, g_ssem, g_rsem, gs_ssem, gs_rsem,
-    a_ssem, a_rsem, b_ssem, b_rsem, z_ssem, z_rsem, cnt_ssem, cnt_rsem,
+    a_ssem, a_rsem, b_ssem, b_rsem, r_ssem, r_rsem, cnt_ssem, cnt_rsem,
     kg_ssem, kg_rsem, f_ssem, f_rsem, fin_ssem, fin_rsem, l_ssem, l_rsem,
 ):
     dp = lax.axis_index("dp")
@@ -88,6 +88,12 @@
     x_ids = [dev(x=k) for k in x_of]
     sib = dev(c=1 - c)
     plane_ids = [dev(x=lax.rem(x + dx, NX), z=lax.rem(z + dz, NZ)) for dx, dz in PLANE]
+    px_ids = [plane_ids[i] for i in range(NP) if PLANE[i][1] % NZL == 0]
+    step2 = 2 + 4 * c
+    near = [lax.rem(z + step, NZ) for step in (step2, 1, 7)]
+    near_ids = [dev(z=k) for k in near]
+    near_cross_ids = [dev(z=k, c=1 - c) for k in near]
+    far_cross_ids = near_cross_ids + [dev(z=lax.rem(z + 8 - step2, NZ), c=1 - c)]
     cross_ids = [xc_ids[i] for i in range(7) if XC[i][0] and XC[i][1]]
 
     def remote(src, dst, ssem, rsem, to):
@@ -103,10 +109,10 @@
 
     barrier = pltpu.get_barrier_semaphore()
     load_tok = pltpu.make_async_copy(tok_ref, tok, load_sem.at[0])
-    load_key = pltpu.make_async_copy(proto_ref.at[:, zl * NC + c], kraw, load_sem.at[1])
+    load_key = pltpu.make_async_copy(proto_ref, kraw, load_sem.at[1])
     load_tok.start()
     load_key.start()
-    for to in [sib] + plane_ids + cross_ids + y_ids:
+    for to in [sib] + plane_ids + cross_ids + far_cross_ids + y_ids:
         pl.semaphore_signal(barrier, inc=1, device_id=to, device_id_type=MESH)
 
     off = off_ref[...].astype(F32)
@@ -115,39 +121,55 @@
     first = jnp.broadcast_to(off_row, (128, 128)).T.astype(jnp.int32)
     row = lax.broadcasted_iota(jnp.int32, (128, 128), 0)
     first = first + (row & 63) * SEQ
+    for part in range(16):
+        col = part * 128
+        inside = (lane + col >= first) & (lane + col < first + CROP)
+        mask[:, pl.ds(col, 128)] = jnp.where(inside, 1.0, 0.0).astype(BF16)
     load_tok.wait()
-    total = jnp.zeros((128, FEAT), F32)
-    for part in range(4):
-        mask = jnp.concatenate(
-            [
-                jnp.where((lane + col >= first) & (lane + col < first + CROP), 1.0, 0.0).astype(BF16)
-                for col in range(part * 512, part * 512 + 512, 128)
-            ],
-            axis=1,
-        )
-        total = total + mm(mask, tok[pl.ds(part * 512, 512)])
+    total = mm(mask[...], tok[...])
     rows = total / CROP
     pooled[...] = rows
-    query = (rows * unit_scale(rows) / math.sqrt(FEAT)).astype(BF16).astype(F32)
-    qg[c, zl, pl.ds(0, 128)] = query
+    query = (rows * unit_scale(rows) / math.sqrt(FEAT)).astype(BF16)
+    qg[c, zl, pl.ds(0, 128)] = query.astype(F32)
     spec = spec_ref[...].astype(F32)
     both = jnp.concatenate([spec, spec], axis=1)
     half = lax.broadcasted_iota(jnp.int32, (8, 128), 1) // 64
     qg[c, zl, pl.ds(128, 8)] = jnp.where(half == c, jnp.broadcast_to(both, (8, 128)), 0.0)
 
-    pl.semaphore_wait(barrier, 11 + NP)
-    step2 = 2 + 4 * c
+    load_key.wait()
+
+    def normalise(i, carry):
+        at = pl.ds(pl.multiple_of(i * 256, 256), 256)
+        raw = kraw[at].astype(F32)
+        kunit[at] = (raw * unit_scale(raw) / math.sqrt(FEAT)).astype(BF16)
+        return carry
+
+    lax.fori_loop(0, 32, normalise, 0)
+    pl.semaphore_wait(barrier, 15 + NP)
+
     mine = qg.at[c, zl]
-    for i, to in enumerate((dev(z=lax.rem(z + step2, NZ)), dev(z=lax.rem(z + 1, NZ)), dev(z=lax.rem(z + 7, NZ)))):
+    for i, to in enumerate(near_ids):
         remote(mine, mine, g_ssem, g_rsem.at[i], to).start()
     remote(mine, mine, gs_ssem, gs_rsem.at[0], sib).start()
 
-    load_key.wait()
+    def whole(i, sums):
+        at = pl.ds(pl.multiple_of(i * 256, 256), 256)
+        e = jnp.exp(mm(kunit[at], query, NT) * 10.0)
+        k = (e * e).astype(BF16).astype(F32)
+        fold = lambda a: jnp.sum(a.reshape(32, 8, 128), axis=0)
+        return sums[0] + fold(k), sums[1] + fold(e)
+
+    zero = jnp.zeros((8, 128), F32)
+    ks, es = lax.fori_loop(0, 32, whole, (zero, zero), unroll=2)
+    r_src[:, pl.ds(0, 128)] = jnp.sum(ks, axis=0, keepdims=True)
+    r_src[:, pl.ds(128, 128)] = jnp.sum(es, axis=0, keepdims=True)
+    for i, to in enumerate(px_ids):
+        remote(r_src, r_px.at[i], r_ssem.at[0], r_rsem.at[0], to).start()
+
     for i in range(8):
-        raw = kraw[i].astype(F32)
-        unit = raw * unit_scale(raw) / math.sqrt(FEAT)
-        keys[pl.ds(i * 128, 128)] = unit.astype(BF16)
-        turned = unit.astype(BF16).astype(F32).T.astype(BF16)
+        block = kunit[pl.ds(pl.multiple_of((i * 8 + zl * NC + c) * 128, 128), 128)]
+        keys[pl.ds(i * 128, 128)] = block
+        turned = block.astype(F32).T.astype(BF16)
         keys_t[:, pl.ds(i * 128, 128)] = turned
         keys_t[:, pl.ds(1024 + i * 128, 128)] = turned
 
@@ -160,7 +182,7 @@
             pair.append(q)
         rhs = jnp.concatenate(pair, axis=0)
 
-        def block(kb, sums):
+        def block(kb, carry):
             k0 = pl.multiple_of(kb * 128, 128)
             s = mm(keys[pl.ds(k0, 128)], rhs, NT)
             e = jnp.exp(s * 10.0)
@@ -170,26 +192,45 @@
                 s_buf[at] = s[:, v * 128 : v * 128 + 128]
                 e_buf[at] = e[:, v * 128 : v * 128 + 128]
                 k_buf[at] = k[:, v * 128 : v * 128 + 128]
-            fold = lambda a: jnp.sum(a.reshape(16, 8, 256), axis=0)
-            return sums[0] + fold(e), sums[1] + fold(k.astype(F32))
-
-        zero = jnp.zeros((8, 256), F32)
-        es, ks = lax.fori_loop(0, 8, block, (zero, zero))
-        es = jnp.sum(es, axis=0, keepdims=True)
-        ks = jnp.sum(ks, axis=0, keepdims=True)
-        for v in range(2):
-            z_src[0, :, pl.ds(v * 512 + zp128, 128)] = es[:, v * 128 : v * 128 + 128]
-            a_src[0, 0, :, pl.ds(v * 512 + zp128, 128)] = ks[:, v * 128 : v * 128 + 128] * (1.0 / PROTOS)
+            return carry
+
+        lax.fori_loop(0, 8, block, 0)
 
     got(qg.at[1 - c, zl], gs_rsem.at[0])
     scores(zl)
-    for i, step in ((1, 3), (2, 1), (0, 2)):
+
+    def member(i, step):
         zp = lax.rem(zl + step, NZL)
         piece = qg.at[c, zp]
         got(piece, g_rsem.at[i])
         remote(piece, piece, gs_ssem, gs_rsem.at[i + 1], sib).start()
         got(qg.at[1 - c, zp], gs_rsem.at[i + 1])
         scores(zp)
+
+    member(1, 3)
+    member(2, 1)
+    got(r_px, r_rsem.at[0])
+    part = r_src[...]
+    for i in range(7):
+        part = part + r_px[i]
+    mine = r_mem.at[c, zl]
+    r_mem[c, zl] = part
+    for to in [sib] + near_ids + near_cross_ids:
+        remote(mine, mine, r_ssem.at[1], r_rsem.at[1], to).start()
+    member(0, 2)
+    got(r_px, r_rsem.at[1])
+    pairs = [[r_mem[i, j] for i in range(2)] for j in range(NZL)]
+
+    def assemble(base):
+        tiles = []
+        for v in range(2):
+            at = base + v * 64
+            for j in range(NZL):
+                tiles += [pairs[j][0][:, at : at + 64], pairs[j][1][:, at : at + 64]]
+        return jnp.concatenate(tiles, axis=1)
+
+    window_scale = PROTOS / assemble(0)
+    totals = assemble(128)
 
     spec_row = jnp.concatenate([qg[0, i, pl.ds(128, 1)] + qg[1, i, pl.ds(128, 1)] for i in range(4)], axis=1)
     group = lax.broadcasted_iota(jnp.int32, (NGROUP, 512), 0)
@@ -227,15 +268,6 @@
         for i, to in enumerate(y_ids):
             remote(cnt_src, cnt_y.at[i], cnt_ssem, cnt_rsem, to).start()
 
-    def z_first():
-        remote(z_src.at[0], z_c, z_ssem.at[0], z_rsem.at[0], sib).start()
-
-    def z_second():
-        got(z_c, z_rsem.at[0])
-        z_src[1] = z_src[0] + z_c[...]
-        for i, to in enumerate(plane_ids):
-            remote(z_src.at[1], z_pl.at[i], z_ssem.at[1], z_rsem.at[1], to).start()
-
     def halves(value, k0, width):
         hi = value.astype(BF16)
         two[pl.ds(k0, width)] = hi
@@ -305,26 +337,17 @@
         send_counts()
         q_core(0)
 
-    def beside_b0():
-        z_first()
-        q_x(0)
-
-    def beside_b1():
-        z_second()
-        q_z(0)
-
+    columns(0, window_scale)
+    proto_scale = 1.0 / (PROTOS * b_sum(0))
+    row_sums(0, proto_scale)
     window_scale = 1.0 / a_sum(0, None, beside_a0)
-    columns(0, window_scale)
-    proto_scale = 1.0 / (PROTOS * b_sum(0, beside_b0))
+    columns(1, window_scale)
+    proto_scale = 1.0 / (PROTOS * b_sum(1, lambda: q_x(0)))
     row_sums(1, proto_scale)
     window_scale = 1.0 / a_sum(1)
-    columns(1, window_scale)
-    proto_scale = 1.0 / (PROTOS * b_sum(1, beside_b1))
+    columns(2, window_scale)
+    proto_scale = 1.0 / (PROTOS * b_sum(2, lambda: q_z(0)))
     row_sums(2, proto_scale)
-    window_scale = 1.0 / a_sum(2)
-    columns(2, window_scale)
-    proto_scale = 1.0 / (PROTOS * b_sum(2))
-    row_sums(3, proto_scale)
     p_row[...] = proto_scale
 
     def cross():
@@ -343,12 +366,8 @@
         q_x(1)
         cross()
 
-    last = 1.0 / a_sum(3, None, beside_a3)
-
-    got(z_pl, z_rsem.at[1])
-    totals = z_src[1]
-    for i in range(NP):
-        totals = totals + z_pl[i]
+    last = 1.0 / a_sum(2, None, beside_a3)
+
     got(cnt_y, cnt_rsem)
     counts = cnt_src[...]
     for i in range(7):
@@ -435,7 +454,8 @@
     for i, k in ((0, 4), (1, 5), (2, 6), (3, 7)):
         got(kg_y.at[i], kg_rsem.at[k])
         part = part + kg_y[i]
-    pgrad_ref[...] = unit_back(kraw[y].astype(F32), part)
+    own = pl.multiple_of((y * 8 + zl * NC + c) * 128, 128)
+    pgrad_ref[...] = unit_back(kraw[pl.ds(own, 128)].astype(F32), part)
 
     got(w_rcv.at[0], fin_rsem)
     for v in range(2):
@@ -449,13 +469,13 @@
 
     sent(qg.at[0, pl.ds(0, 3)], g_ssem)
     sent(qg.at[0], gs_ssem)
-    for it in range(4):
+    for it in range(3):
         sent(a_c.at[it], a_ssem.at[it, 0])
         sent(a_pl.at[it], a_ssem.at[it, 1])
     for it in range(3):
         sent(b_y.at[it], b_ssem.at[it])
-    sent(z_c, z_ssem.at[0])
-    sent(z_pl, z_ssem.at[1])
+    sent(r_px, r_ssem.at[0])
+    sent(r_px, r_ssem.at[1])
     sent(cnt_y, cnt_ssem)
     for i in range(2):
         sent(kg_half.at[i], kg_ssem.at[i])
@@ -470,6 +490,15 @@
         sent(l_xc.at[pl.ds(0, 7)], l_ssem.at[i])
 
 
+def hand_on(view_in, pgrad_in, loss_in, view_ref, pgrad_ref, loss_ref, sem):
+    pairs = ((view_in, view_ref), (pgrad_in, pgrad_ref), (loss_in, loss_ref))
+    copies = [pltpu.make_async_copy(src, dst, sem.at[i]) for i, (src, dst) in enumerate(pairs)]
+    for copy in copies:
+        copy.start()
+    for copy in copies:
+        copy.wait()
+
+
 def on_device(tokens, offsets, species, prototypes):
     vmem = pltpu.VMEM
     dma = pltpu.SemaphoreType.DMA
@@ -477,7 +506,9 @@
     inside = pl.BlockSpec(memory_space=pltpu.VMEM)
     scratch = [
         vmem((64 * SEQ, FEAT), BF16),
-        vmem((8, 128, FEAT), BF16),
+        vmem((128, 64 * SEQ), BF16),
+        vmem((8192, FEAT), BF16),
+        vmem((8192, FEAT), BF16),
         vmem((1024, FEAT), BF16),
         vmem((FEAT, 2048), BF16),
         vmem((128, FEAT), F32),
@@ -488,14 +519,14 @@
         vmem((2, 1024, 512), BF16),
         vmem((2, 1024, 512), F32),
         vmem((2048, 512), BF16),
-        vmem((4, 2, 1, 1024), F32),
-        vmem((4, 1, 1024), F32),
-        vmem((4, NP, 1, 1024), F32),
+        vmem((3, 2, 1, 1024), F32),
+        vmem((3, 1, 1024), F32),
+        vmem((3, NP, 1, 1024), F32),
         vmem((3, 1, 2048), F32),
         vmem((3, 7, 1, 2048), F32),
-        vmem((2, 1, 1024), F32),
-        vmem((1, 1024), F32),
-        vmem((NP, 1, 1024), F32),
+        vmem((1, 256), F32),
+        vmem((7, 1, 256), F32),
+        vmem((2, 4, 1, 256), F32),
         vmem((NGROUP, 128), F32),
         vmem((7, NGROUP, 128), F32),
         vmem((8, 128, FEAT), F32),
@@ -518,7 +549,7 @@
         vmem((2, 128, FEAT), F32),
         dma((2,)),
         dma, dma((3,)), dma, dma((4,)),
-        dma((4, 2)), dma((4, 2)), dma((3,)), dma((3,)), dma((2,)), dma((2,)), dma, dma,
+        dma((3, 2)), dma((3, 2)), dma((3,)), dma((3,)), dma((2,)), dma((2,)), dma, dma,
         dma((8,)), dma((8,)), dma((2, 3)), dma((2, 3)), dma, dma, dma((3,)), dma((3,)),
     ]
     view_grads, proto_grads, loss = pl.pallas_call(
@@ -539,8 +570,21 @@
         tokens.reshape(64 * SEQ, FEAT),
         offsets,
         species.reshape(1, 64),
-        prototypes.reshape(8, 8, 128, FEAT),
+        prototypes,
     )
+    view_grads, proto_grads, loss = pl.pallas_call(
+        hand_on,
+        out_shape=(
+            jax.ShapeDtypeStruct((2, 64, FEAT), F32),
+            jax.ShapeDtypeStruct((128, FEAT), F32),
+            jax.ShapeDtypeStruct((1, 1), F32),
+        ),
+        in_specs=[anywhere] * 3,
+        out_specs=(anywhere, anywhere, anywhere),
+        scratch_shapes=[dma((3,))],
+        compiler_params=pltpu.CompilerParams(vmem_limit_bytes=60 * 2**20),
+        name="results",
+    )(view_grads, proto_grads, loss)
     return view_grads, proto_grads, loss.reshape(())
 
 

time: 95.7 us -> 92 us (0.961)
  local copies, waits for them, and re-layouts: 2.95 us -> 0 us
  between operations: 2.45 us -> 0.64 us
    pallas_call x0 -> x1, Pallas kernels: none -> 5.72 us  [on_device(): pl.pallas_call(hand_on, out_shape=(jax.ShapeDtypeStruct((2, 64, FEAT), F3...]
    pallas_call x1, Pallas kernels: 90 us -> 85.2 us  [on_device(): pl.pallas_call(kernel, out_shape=(jax.ShapeDtypeStruct((2, 64, FEAT), F32...]
    unnamed x2 -> x0, local copies, waits for them, and re-layouts: 2.95 us -> none
where the time goes in v3:
time: 92 us; the launch traced here: 91.6 us
  Pallas kernels  90.9 us (99%)
    pallas_call x1, Pallas kernels, on_device(): pl.pallas_call(kernel, out_shape=(jax.ShapeDtypeStruct((2, 64, FEAT), F32...  85.2 us
    pallas_call x1, Pallas kernels, on_device(): pl.pallas_call(hand_on, out_shape=(jax.ShapeDtypeStruct((2, 64, FEAT), F3...  5.72 us

profile of v3, /device:TPU:1, one launch (start us, length us, event | category | flops | bytes accessed | tf_op | source)
XLA Modules:
  0.0 91.6 jit_solution(16545947506150600857)
XLA Ops:
  0.6 85.2 %swav_step.1 = (f32[2,64,128]{2,1,0:T(8,128)}, f32[128,128]{1,0:T(8,128)}, f32[1,1]{1,0:T(1,128)}) custom-call(bf16[2048,128]{1,0:T(8,128)(2,1)} %bitcast.3, s32[2,64]{1,0:T(2,128)} %off_ref.1, s32[1,64]{1,0:T(1,128)} %bitcast.4, bf16[8192,128]{1,0:T(8,128)(2,1)} %proto_ref.1), custom_call_target="tpu_custom_call" | custom-call | tf_op jit(solution)/shard_map/swav_step/pallas_call | solution.py:555
  85.8 5.7 %results.1 = (f32[2,64,128]{2,1,0:T(8,128)}, f32[128,128]{1,0:T(8,128)}, f32[1,1]{1,0:T(1,128)}) custom-call(f32[2,64,128]{2,1,0:T(8,128)} %get-tuple-element.9.view_in, f32[128,128]{1,0:T(8,128)} %get-tuple-element.10.pgrad_in, f32[1,1]{1,0:T(1,128)} %get-tuple-element.11.loss_in), custom_call_target="tpu_custom_call" | custom-call | tf_op jit(solution)/shard_map/results/pallas_call | solution.py:575

commit v4 on v3

--- a/solution.py
+++ b/solution.py
@@ -139,12 +139,12 @@
     load_key.wait()
 
     def normalise(i, carry):
-        at = pl.ds(pl.multiple_of(i * 256, 256), 256)
+        at = pl.ds(pl.multiple_of(i * 2048, 2048), 2048)
         raw = kraw[at].astype(F32)
-        kunit[at] = (raw * unit_scale(raw) / math.sqrt(FEAT)).astype(BF16)
+        kunit[at] = (raw * (unit_scale(raw) * (1.0 / math.sqrt(FEAT)))).astype(BF16)
         return carry
 
-    lax.fori_loop(0, 32, normalise, 0)
+    lax.fori_loop(0, 4, normalise, 0)
     pl.semaphore_wait(barrier, 15 + NP)
 
     mine = qg.at[c, zl]
@@ -153,14 +153,14 @@
     remote(mine, mine, gs_ssem, gs_rsem.at[0], sib).start()
 
     def whole(i, sums):
-        at = pl.ds(pl.multiple_of(i * 256, 256), 256)
+        at = pl.ds(pl.multiple_of(i * 4096, 4096), 4096)
         e = jnp.exp(mm(kunit[at], query, NT) * 10.0)
         k = (e * e).astype(BF16).astype(F32)
-        fold = lambda a: jnp.sum(a.reshape(32, 8, 128), axis=0)
+        fold = lambda a: jnp.sum(a.reshape(512, 8, 128), axis=0)
         return sums[0] + fold(k), sums[1] + fold(e)
 
     zero = jnp.zeros((8, 128), F32)
-    ks, es = lax.fori_loop(0, 32, whole, (zero, zero), unroll=2)
+    ks, es = lax.fori_loop(0, 2, whole, (zero, zero))
     r_src[:, pl.ds(0, 128)] = jnp.sum(ks, axis=0, keepdims=True)
     r_src[:, pl.ds(128, 128)] = jnp.sum(es, axis=0, keepdims=True)
     for i, to in enumerate(px_ids):
@@ -182,19 +182,14 @@
             pair.append(q)
         rhs = jnp.concatenate(pair, axis=0)
 
-        def block(kb, carry):
-            k0 = pl.multiple_of(kb * 128, 128)
-            s = mm(keys[pl.ds(k0, 128)], rhs, NT)
-            e = jnp.exp(s * 10.0)
-            k = (e * e).astype(BF16)
-            for v in range(2):
-                at = (v, pl.ds(k0, 128), pl.ds(zp128, 128))
-                s_buf[at] = s[:, v * 128 : v * 128 + 128]
-                e_buf[at] = e[:, v * 128 : v * 128 + 128]
-                k_buf[at] = k[:, v * 128 : v * 128 + 128]
-            return carry
-
-        lax.fori_loop(0, 8, block, 0)
+        out = mm(keys[...], rhs, NT)
+        e = jnp.exp(out * 10.0)
+        k = (e * e).astype(BF16)
+        for v in range(2):
+            at = (v, slice(None), pl.ds(zp128, 128))
+            s_buf[at] = out[:, v * 128 : v * 128 + 128]
+            e_buf[at] = e[:, v * 128 : v * 128 + 128]
+            k_buf[at] = k[:, v * 128 : v * 128 + 128]
 
     got(qg.at[1 - c, zl], gs_rsem.at[0])
     scores(zl)
@@ -490,13 +485,10 @@
         sent(l_xc.at[pl.ds(0, 7)], l_ssem.at[i])
 
 
-def hand_on(view_in, pgrad_in, loss_in, view_ref, pgrad_ref, loss_ref, sem):
-    pairs = ((view_in, view_ref), (pgrad_in, pgrad_ref), (loss_in, loss_ref))
-    copies = [pltpu.make_async_copy(src, dst, sem.at[i]) for i, (src, dst) in enumerate(pairs)]
-    for copy in copies:
-        copy.start()
-    for copy in copies:
-        copy.wait()
+def hand_on(view_in, pgrad_in, loss_in, view_ref, pgrad_ref, loss_ref):
+    view_ref[...] = view_in[...]
+    pgrad_ref[...] = pgrad_in[...]
+    loss_ref[...] = loss_in[...]
 
 
 def on_device(tokens, offsets, species, prototypes):
@@ -579,9 +571,8 @@
             jax.ShapeDtypeStruct((128, FEAT), F32),
             jax.ShapeDtypeStruct((1, 1), F32),
         ),
-        in_specs=[anywhere] * 3,
-        out_specs=(anywhere, anywhere, anywhere),
-        scratch_shapes=[dma((3,))],
+        in_specs=[inside] * 3,
+        out_specs=(inside, inside, inside),
         compiler_params=pltpu.CompilerParams(vmem_limit_bytes=60 * 2**20),
         name="results",
     )(view_grads, proto_grads, loss)

time: 92 us -> 84.9 us (0.923)
  Pallas kernels: 90.9 us -> 84.1 us
    pallas_call x1, Pallas kernels: 5.72 us -> 2.15 us  [on_device(): pl.pallas_call(hand_on, out_shape=(jax.ShapeDtypeStruct((2, 64, FEAT), F3...]
    pallas_call x1, Pallas kernels: 85.2 us -> 81.9 us  [on_device(): pl.pallas_call(kernel, out_shape=(jax.ShapeDtypeStruct((2, 64, FEAT), F32...]
where the time goes in v4:
time: 84.9 us; the launch traced here: 84.7 us
  Pallas kernels  84.1 us (99%)
    pallas_call x1, Pallas kernels, on_device(): pl.pallas_call(kernel, out_shape=(jax.ShapeDtypeStruct((2, 64, FEAT), F32...  81.9 us
    pallas_call x1, Pallas kernels, on_device(): pl.pallas_call(hand_on, out_shape=(jax.ShapeDtypeStruct((2, 64, FEAT), F3...  2.15 us

profile of v4, /device:TPU:1, one launch (start us, length us, event | category | flops | bytes accessed | tf_op | source)
XLA Modules:
  0.0 84.7 jit_solution(17767616345274552020)
XLA Ops:
  0.6 81.9 %swav_step.1 = (f32[2,64,128]{2,1,0:T(8,128)}, f32[128,128]{1,0:T(8,128)}, f32[1,1]{1,0:T(1,128)}) custom-call(bf16[2048,128]{1,0:T(8,128)(2,1)} %bitcast.3, s32[2,64]{1,0:T(2,128)} %off_ref.1, s32[1,64]{1,0:T(1,128)} %bitcast.4, bf16[8192,128]{1,0:T(8,128)(2,1)} %proto_ref.1), custom_call_target="tpu_custom_call" | custom-call | tf_op jit(solution)/shard_map/swav_step/pallas_call | solution.py:547
  82.5 2.2 %results.1 = (f32[2,64,128]{2,1,0:T(8,128)}, f32[128,128]{1,0:T(8,128)}, f32[1,1]{1,0:T(1,128)}) custom-call(f32[2,64,128]{2,1,0:T(8,128)} %get-tuple-element.9.view_in, f32[128,128]{1,0:T(8,128)} %get-tuple-element.10.pgrad_in, f32[1,1]{1,0:T(1,128)} %get-tuple-element.11.loss_in), custom_call_target="tpu_custom_call" | custom-call | tf_op jit(solution)/shard_map/results/pallas_call | solution.py:567

commit v5 on v4

--- a/solution.py
+++ b/solution.py
@@ -62,8 +62,8 @@
 def kernel(
     tok_ref, off_ref, spec_ref, proto_ref,
     view_ref, pgrad_ref, loss_ref,
-    tok, mask, kraw, kunit, keys, keys_t, pooled, qg, q16, s_buf, e_buf, k_buf, t_buf, two,
-    a_src, a_c, a_pl, b_src, b_y, r_src, r_px, r_mem, cnt_src, cnt_y,
+    tok, mask, kraw, kunit, keys, keys_t, pooled, qg, q16, s_buf, e_buf, k_buf, kt_buf, t_buf, two,
+    a_src, a_c, a_pl, b_src, b_y, r_two, r_pl, r_mem, cnt_src, cnt_y,
     kg_src, kg_half, kg_fwd, kg_y, c_src, c_rcv, x_src, x_rcv, w_src, w_rcv, fin, l_xc, l_z, l_y,
     x_rows, p_row, ab_rows, qt,
     load_sem, g_ssem, g_rsem, gs_ssem, gs_rsem,
@@ -88,12 +88,9 @@
     x_ids = [dev(x=k) for k in x_of]
     sib = dev(c=1 - c)
     plane_ids = [dev(x=lax.rem(x + dx, NX), z=lax.rem(z + dz, NZ)) for dx, dz in PLANE]
-    px_ids = [plane_ids[i] for i in range(NP) if PLANE[i][1] % NZL == 0]
     step2 = 2 + 4 * c
     near = [lax.rem(z + step, NZ) for step in (step2, 1, 7)]
     near_ids = [dev(z=k) for k in near]
-    near_cross_ids = [dev(z=k, c=1 - c) for k in near]
-    far_cross_ids = near_cross_ids + [dev(z=lax.rem(z + 8 - step2, NZ), c=1 - c)]
     cross_ids = [xc_ids[i] for i in range(7) if XC[i][0] and XC[i][1]]
 
     def remote(src, dst, ssem, rsem, to):
@@ -112,7 +109,7 @@
     load_key = pltpu.make_async_copy(proto_ref, kraw, load_sem.at[1])
     load_tok.start()
     load_key.start()
-    for to in [sib] + plane_ids + cross_ids + far_cross_ids + y_ids:
+    for to in plane_ids + y_ids + cross_ids + [sib]:
         pl.semaphore_signal(barrier, inc=1, device_id=to, device_id_type=MESH)
 
     off = off_ref[...].astype(F32)
@@ -145,13 +142,6 @@
         return carry
 
     lax.fori_loop(0, 4, normalise, 0)
-    pl.semaphore_wait(barrier, 15 + NP)
-
-    mine = qg.at[c, zl]
-    for i, to in enumerate(near_ids):
-        remote(mine, mine, g_ssem, g_rsem.at[i], to).start()
-    remote(mine, mine, gs_ssem, gs_rsem.at[0], sib).start()
-
     def whole(i, sums):
         at = pl.ds(pl.multiple_of(i * 4096, 4096), 4096)
         e = jnp.exp(mm(kunit[at], query, NT) * 10.0)
@@ -161,10 +151,20 @@
 
     zero = jnp.zeros((8, 128), F32)
     ks, es = lax.fori_loop(0, 2, whole, (zero, zero))
-    r_src[:, pl.ds(0, 128)] = jnp.sum(ks, axis=0, keepdims=True)
-    r_src[:, pl.ds(128, 128)] = jnp.sum(es, axis=0, keepdims=True)
-    for i, to in enumerate(px_ids):
-        remote(r_src, r_px.at[i], r_ssem.at[0], r_rsem.at[0], to).start()
+    r_two[c, :, pl.ds(0, 128)] = jnp.sum(ks, axis=0, keepdims=True)
+    r_two[c, :, pl.ds(128, 128)] = jnp.sum(es, axis=0, keepdims=True)
+
+    pl.semaphore_wait(barrier, 11 + NP)
+    remote(r_two.at[c], r_two.at[c], r_ssem.at[0], r_rsem.at[0], sib).start()
+
+    mine = qg.at[c, zl]
+    for i, to in enumerate(near_ids):
+        remote(mine, mine, g_ssem, g_rsem.at[i], to).start()
+    remote(mine, mine, gs_ssem, gs_rsem.at[0], sib).start()
+
+    got(r_two.at[1 - c], r_rsem.at[0])
+    for i, to in enumerate(plane_ids):
+        remote(r_two, r_pl.at[i], r_ssem.at[1], r_rsem.at[1], to).start()
 
     for i in range(8):
         block = kunit[pl.ds(pl.multiple_of((i * 8 + zl * NC + c) * 128, 128), 128)]
@@ -204,17 +204,15 @@
 
     member(1, 3)
     member(2, 1)
-    got(r_px, r_rsem.at[0])
-    part = r_src[...]
-    for i in range(7):
-        part = part + r_px[i]
-    mine = r_mem.at[c, zl]
-    r_mem[c, zl] = part
-    for to in [sib] + near_ids + near_cross_ids:
-        remote(mine, mine, r_ssem.at[1], r_rsem.at[1], to).start()
     member(0, 2)
-    got(r_px, r_rsem.at[1])
-    pairs = [[r_mem[i, j] for i in range(2)] for j in range(NZL)]
+    got(r_pl, r_rsem.at[1])
+    for step in range(NZL):
+        part = r_two[...] if step == 0 else None
+        for i, (dx, dz) in enumerate(PLANE):
+            if dz % NZL == step:
+                part = r_pl[i] if part is None else part + r_pl[i]
+        r_mem[lax.rem(zl + NZL - step, NZL)] = part
+    pairs = [r_mem[j] for j in range(NZL)]
 
     def assemble(base):
         tiles = []
@@ -284,13 +282,14 @@
             t_buf[v, pl.ds(i * 128, 128)] = t
             halves(t, i * 128, 128)
 
-    def q_core(step):
-        prepare = (split_e, split_t)[step]
+    def q_theirs(step):
         theirs = 1 - c if step == 0 else c
-        prepare(theirs)
+        (split_e, split_t)[step](theirs)
         c_src[step] = mm(keys_t[...], two[...])
         remote(c_src.at[step], c_rcv.at[step], f_ssem.at[step, 0], f_rsem.at[step, 0], sib).start()
-        prepare(1 - theirs)
+
+    def q_own(step):
+        (split_e, split_t)[step](c if step == 0 else 1 - c)
         x_src[step] = mm(keys_t[...], two[...])
 
     def q_x(step):
@@ -320,7 +319,8 @@
 
     def columns(it, scale):
         for v in range(2):
-            out = mm(split3(scale[:, v * 512 : v * 512 + 512]), k_buf[v], NT)
+            parts = split3(scale[:, v * 512 : v * 512 + 512])
+            out = mm(parts, k_buf[v], NT) if it == 0 else mm(parts, kt_buf[v])
             b_src[it, :, pl.ds(v * 1024, 1024)] = jnp.sum(out, axis=0, keepdims=True)
 
     def row_sums(it, scale):
@@ -330,10 +330,15 @@
 
     def beside_a0():
         send_counts()
-        q_core(0)
+        q_theirs(0)
+        q_own(0)
+
+    def turn():
+        for v in range(2):
+            kt_buf[v] = k_buf[v].T
 
     columns(0, window_scale)
-    proto_scale = 1.0 / (PROTOS * b_sum(0))
+    proto_scale = 1.0 / (PROTOS * b_sum(0, turn))
     row_sums(0, proto_scale)
     window_scale = 1.0 / a_sum(0, None, beside_a0)
     columns(1, window_scale)
@@ -356,12 +361,12 @@
             acc = lax.fori_loop(0, 32, block, jnp.zeros((8, 512), F32))
             x_rows[v] = jnp.sum(acc, axis=0, keepdims=True)
 
-    def beside_a3():
-        q_core(1)
+    def beside_a2():
+        q_own(1)
         q_x(1)
         cross()
 
-    last = 1.0 / a_sum(2, None, beside_a3)
+    last = 1.0 / a_sum(2, lambda: q_theirs(1), beside_a2)
 
     got(cnt_y, cnt_rsem)
     counts = cnt_src[...]
@@ -469,8 +474,8 @@
         sent(a_pl.at[it], a_ssem.at[it, 1])
     for it in range(3):
         sent(b_y.at[it], b_ssem.at[it])
-    sent(r_px, r_ssem.at[0])
-    sent(r_px, r_ssem.at[1])
+    sent(r_two.at[0], r_ssem.at[0])
+    sent(r_pl, r_ssem.at[1])
     sent(cnt_y, cnt_ssem)
     for i in range(2):
         sent(kg_half.at[i], kg_ssem.at[i])
@@ -509,6 +514,7 @@
         vmem((2, 1024, 512), F32),
         vmem((2, 1024, 512), F32),
         vmem((2, 1024, 512), BF16),
+        vmem((2, 512, 1024), BF16),
         vmem((2, 1024, 512), F32),
         vmem((2048, 512), BF16),
         vmem((3, 2, 1, 1024), F32),
@@ -516,9 +522,9 @@
         vmem((3, NP, 1, 1024), F32),
         vmem((3, 1, 2048), F32),
         vmem((3, 7, 1, 2048), F32),
-        vmem((1, 256), F32),
-        vmem((7, 1, 256), F32),
-        vmem((2, 4, 1, 256), F32),
+        vmem((2, 1, 256), F32),
+        vmem((NP, 2, 1, 256), F32),
+        vmem((4, 2, 1, 256), F32),
         vmem((NGROUP, 128), F32),
         vmem((7, NGROUP, 128), F32),
         vmem((8, 128, FEAT), F32),

time: 84.9 us -> 83.2 us (0.980); the launches traced: 84.7 us -> 81.7 us
  Pallas kernels: 84.1 us -> 81.1 us
    pallas_call x1, Pallas kernels: 81.9 us -> 78.9 us  [on_device(): pl.pallas_call(kernel, out_shape=(jax.ShapeDtypeStruct((2, 64, FEAT), F32...]
where the time goes in v5:
time: 83.2 us; the launch traced here: 81.7 us
  Pallas kernels  81.1 us (97%)
    pallas_call x1, Pallas kernels, on_device(): pl.pallas_call(kernel, out_shape=(jax.ShapeDtypeStruct((2, 64, FEAT), F32...  78.9 us
    pallas_call x1, Pallas kernels, on_device(): pl.pallas_call(hand_on, out_shape=(jax.ShapeDtypeStruct((2, 64, FEAT), F3...  2.15 us

profile of v5, /device:TPU:1, one launch (start us, length us, event | category | flops | bytes accessed | tf_op | source)
XLA Modules:
  0.0 81.7 jit_solution(110113066243775837)
XLA Ops:
  0.6 78.9 %swav_step.1 = (f32[2,64,128]{2,1,0:T(8,128)}, f32[128,128]{1,0:T(8,128)}, f32[1,1]{1,0:T(1,128)}) custom-call(bf16[2048,128]{1,0:T(8,128)(2,1)} %bitcast.3, s32[2,64]{1,0:T(2,128)} %off_ref.1, s32[1,64]{1,0:T(1,128)} %bitcast.4, bf16[8192,128]{1,0:T(8,128)(2,1)} %proto_ref.1), custom_call_target="tpu_custom_call" | custom-call | tf_op jit(solution)/shard_map/swav_step/pallas_call | solution.py:553
  79.6 2.2 %results.1 = (f32[2,64,128]{2,1,0:T(8,128)}, f32[128,128]{1,0:T(8,128)}, f32[1,1]{1,0:T(1,128)}) custom-call(f32[2,64,128]{2,1,0:T(8,128)} %get-tuple-element.9.view_in, f32[128,128]{1,0:T(8,128)} %get-tuple-element.10.pgrad_in, f32[1,1]{1,0:T(1,128)} %get-tuple-element.11.loss_in), custom_call_target="tpu_custom_call" | custom-call | tf_op jit(solution)/shard_map/results/pallas_call | solution.py:573

commit v6 on v5

--- a/solution.py
+++ b/solution.py
@@ -63,9 +63,9 @@
     tok_ref, off_ref, spec_ref, proto_ref,
     view_ref, pgrad_ref, loss_ref,
     tok, mask, kraw, kunit, keys, keys_t, pooled, qg, q16, s_buf, e_buf, k_buf, kt_buf, t_buf, two,
-    a_src, a_c, a_pl, b_src, b_y, r_two, r_pl, r_mem, cnt_src, cnt_y,
-    kg_src, kg_half, kg_fwd, kg_y, c_src, c_rcv, x_src, x_rcv, w_src, w_rcv, fin, l_xc, l_z, l_y,
-    x_rows, p_row, ab_rows, qt,
+    a_src, a_c, a_pl, b_src, b_y, r_two, r_pl, cnt_src, cnt_y,
+    kg_src, kg_half, kg_fwd, kg_y, c_src, c_rcv, x_src, x_rcv, w_src, w_rcv, fin, l_y,
+    x_own, x_c, x_pl, p_row, ab_rows, qt,
     load_sem, g_ssem, g_rsem, gs_ssem, gs_rsem,
     a_ssem, a_rsem, b_ssem, b_rsem, r_ssem, r_rsem, cnt_ssem, cnt_rsem,
     kg_ssem, kg_rsem, f_ssem, f_rsem, fin_ssem, fin_rsem, l_ssem, l_rsem,
@@ -91,6 +91,7 @@
     step2 = 2 + 4 * c
     near = [lax.rem(z + step, NZ) for step in (step2, 1, 7)]
     near_ids = [dev(z=k) for k in near]
+    here = z * NX + x
     cross_ids = [xc_ids[i] for i in range(7) if XC[i][0] and XC[i][1]]
 
     def remote(src, dst, ssem, rsem, to):
@@ -163,8 +164,9 @@
     remote(mine, mine, gs_ssem, gs_rsem.at[0], sib).start()
 
     got(r_two.at[1 - c], r_rsem.at[0])
-    for i, to in enumerate(plane_ids):
-        remote(r_two, r_pl.at[i], r_ssem.at[1], r_rsem.at[1], to).start()
+    r_pl[here] = r_two[...]
+    for to in plane_ids:
+        remote(r_pl.at[here], r_pl.at[here], r_ssem.at[1], r_rsem.at[1], to).start()
 
     for i in range(8):
         block = kunit[pl.ds(pl.multiple_of((i * 8 + zl * NC + c) * 128, 128), 128)]
@@ -205,14 +207,14 @@
     member(1, 3)
     member(2, 1)
     member(0, 2)
-    got(r_pl, r_rsem.at[1])
-    for step in range(NZL):
-        part = r_two[...] if step == 0 else None
-        for i, (dx, dz) in enumerate(PLANE):
-            if dz % NZL == step:
+    got(r_pl.at[pl.ds(0, NP)], r_rsem.at[1])
+    pairs = []
+    for j in range(NZL):
+        part = None
+        for i in range(NZ * NX):
+            if (i // NX) % NZL == j:
                 part = r_pl[i] if part is None else part + r_pl[i]
-        r_mem[lax.rem(zl + NZL - step, NZL)] = part
-    pairs = [r_mem[j] for j in range(NZL)]
+        pairs.append(part)
 
     def assemble(base):
         tiles = []
@@ -229,21 +231,30 @@
     group = lax.broadcasted_iota(jnp.int32, (NGROUP, 512), 0)
     onehot = jnp.where(group == jnp.broadcast_to(spec_row, (NGROUP, 512)).astype(jnp.int32), 1.0, 0.0)
 
-    def a_sum(it, between_1=None, between_2=None):
-        remote(a_src.at[it, 0], a_c.at[it], a_ssem.at[it, 0], a_rsem.at[it, 0], sib).start()
-        if between_1 is not None:
-            between_1()
+    def plane_sum(own, slots, ssem, rsem, between):
+        slots[here] = own
+        for to in plane_ids:
+            remote(slots.at[here], slots.at[here], ssem, rsem, to).start()
+        between()
+
+        def result():
+            got(slots.at[pl.ds(0, NP)], rsem)
+            part = slots[0]
+            for i in range(1, NP + 1):
+                part = part + slots[i]
+            return part
+
+        return result
+
+    def nothing():
+        pass
+
+    def a_sum(it, between_1=nothing, between_2=nothing):
+        remote(a_src.at[it], a_c.at[it], a_ssem.at[it, 0], a_rsem.at[it, 0], sib).start()
+        between_1()
         got(a_c.at[it], a_rsem.at[it, 0])
-        part = a_src[it, 0] + a_c[it]
-        a_src[it, 1] = part
-        for i, to in enumerate(plane_ids):
-            remote(a_src.at[it, 1], a_pl.at[it, i], a_ssem.at[it, 1], a_rsem.at[it, 1], to).start()
-        if between_2 is not None:
-            between_2()
-        got(a_pl.at[it], a_rsem.at[it, 1])
-        for i in range(NP):
-            part = part + a_pl[it, i]
-        return part
+        part = a_src[it] + a_c[it]
+        return plane_sum(part, a_pl.at[it], a_ssem.at[it, 1], a_rsem.at[it, 1], between_2)()
 
     def b_sum(it, between=None):
         for i, to in enumerate(y_ids):
@@ -295,26 +306,27 @@
     def q_x(step):
         got(c_rcv.at[step], f_rsem.at[step, 0])
         x_src[step] = x_src[step] + c_rcv[step]
-        for i, xx in enumerate(x_of):
-            piece = x_src.at[step, pl.ds(pl.multiple_of(xx * 32, 32), 32)]
-            remote(piece, x_rcv.at[step, i], f_ssem.at[step, 1], f_rsem.at[step, 1], x_ids[i]).start()
-
-    def q_z(step):
-        got(x_rcv.at[step], f_rsem.at[step, 1])
-        part = x_src[step, pl.ds(pl.multiple_of(x * 32, 32), 32)]
+        for h in range(2):
+            for i, xx in enumerate(x_of):
+                piece = x_src.at[step, pl.ds(pl.multiple_of(xx * 32 + h * 16, 16), 16)]
+                remote(piece, x_rcv.at[step, h, i], f_ssem.at[step, 1 + h], f_rsem.at[step, 1 + h], x_ids[i]).start()
+
+    def q_z(step, h):
+        got(x_rcv.at[step, h], f_rsem.at[step, 1 + h])
+        part = x_src[step, pl.ds(pl.multiple_of(x * 32 + h * 16, 16), 16)]
         for i in range(3):
-            part = part + x_rcv[step, i]
+            part = part + x_rcv[step, h, i]
         for i in range(4):
-            w_src[step, i] = part[:, i * 128 : i * 128 + 128]
+            w_src[step, h, i] = part[:, i * 128 : i * 128 + 128]
         for i, to in enumerate(z_ids):
-            piece = w_src.at[step, lax.rem(z_of[i], NZL)]
-            remote(piece, w_rcv.at[step, i], f_ssem.at[step, 2], f_rsem.at[step, 2], to).start()
-
-    def q_end(step):
-        got(w_rcv.at[step], f_rsem.at[step, 2])
-        part = w_src[step, zl]
+            piece = w_src.at[step, h, lax.rem(z_of[i], NZL)]
+            remote(piece, w_rcv.at[step, h, i], f_ssem.at[step, 3 + h], f_rsem.at[step, 3 + h], to).start()
+
+    def q_end(step, h):
+        got(w_rcv.at[step, h], f_rsem.at[step, 3 + h])
+        part = w_src[step, h, zl]
         for i in range(7):
-            part = part + w_rcv[step, i]
+            part = part + w_rcv[step, h, i]
         return part
 
     def columns(it, scale):
@@ -326,7 +338,11 @@
     def row_sums(it, scale):
         for v in range(2):
             out = mm(split3(scale[:, v * 1024 : v * 1024 + 1024]), k_buf[v])
-            a_src[it, 0, :, pl.ds(v * 512, 512)] = jnp.sum(out, axis=0, keepdims=True)
+            a_src[it, :, pl.ds(v * 512, 512)] = jnp.sum(out, axis=0, keepdims=True)
+
+    def both_z():
+        q_z(0, 0)
+        q_z(0, 1)
 
     def beside_a0():
         send_counts()
@@ -340,13 +356,13 @@
     columns(0, window_scale)
     proto_scale = 1.0 / (PROTOS * b_sum(0, turn))
     row_sums(0, proto_scale)
-    window_scale = 1.0 / a_sum(0, None, beside_a0)
+    window_scale = 1.0 / a_sum(0, nothing, beside_a0)
     columns(1, window_scale)
     proto_scale = 1.0 / (PROTOS * b_sum(1, lambda: q_x(0)))
     row_sums(1, proto_scale)
     window_scale = 1.0 / a_sum(1)
     columns(2, window_scale)
-    proto_scale = 1.0 / (PROTOS * b_sum(2, lambda: q_z(0)))
+    proto_scale = 1.0 / (PROTOS * b_sum(2, both_z))
     row_sums(2, proto_scale)
     p_row[...] = proto_scale
 
@@ -359,13 +375,17 @@
                 return acc + jnp.sum(prod.reshape(4, 8, 512), axis=0)
 
             acc = lax.fori_loop(0, 32, block, jnp.zeros((8, 512), F32))
-            x_rows[v] = jnp.sum(acc, axis=0, keepdims=True)
+            x_own[:, pl.ds(v * 512, 512)] = jnp.sum(acc, axis=0, keepdims=True)
 
     def beside_a2():
         q_own(1)
         q_x(1)
         cross()
-
+        remote(x_own, x_c, l_ssem.at[0], l_rsem.at[0], sib).start()
+        got(x_c, l_rsem.at[0])
+        cross_sum.append(plane_sum(x_own[...] + x_c[...], x_pl, l_ssem.at[1], l_rsem.at[1], nothing))
+
+    cross_sum = []
     last = 1.0 / a_sum(2, lambda: q_theirs(1), beside_a2)
 
     got(cnt_y, cnt_rsem)
@@ -381,15 +401,6 @@
     for v in range(2):
         ab_rows[0, v] = a_v[v]
         ab_rows[1, v] = b_v[v]
-    terms = jnp.zeros((1, 512), F32)
-    for v in range(2):
-        terms = terms + 0.5 * weight * (jnp.log(tot_v[v]) / 64.0 - 10.0 * last_v[1 - v] * x_rows[v])
-    terms = terms[:, 0:128] + terms[:, 128:256] + terms[:, 256:384] + terms[:, 384:512]
-    me_xc = x * NC + c
-    l_xc[me_xc] = terms
-    for to in xc_ids:
-        remote(l_xc.at[me_xc], l_xc.at[me_xc], l_ssem.at[0], l_rsem.at[0], to).start()
-
     def add_slots(ref):
         out = ref[0]
         for i in range(1, 8):
@@ -422,7 +433,18 @@
     remote(kg_src.at[7], kg_y.at[1], kg_ssem.at[5], kg_rsem.at[5], down1).start()
     key_part(0, y)
 
-    q_z(1)
+    q_z(1, 0)
+    q_z(1, 1)
+
+    shared = cross_sum[0]()
+    terms = jnp.zeros((1, 512), F32)
+    for v in range(2):
+        x_row = shared[:, v * 512 : v * 512 + 512]
+        terms = terms + 0.5 * weight * (jnp.log(tot_v[v]) - 10.0 * last_v[1 - v] * x_row)
+    l_y[y] = terms[:, 0:128] + terms[:, 128:256] + terms[:, 256:384] + terms[:, 384:512]
+    for to in y_ids:
+        remote(l_y.at[y], l_y.at[y], l_ssem.at[2], l_rsem.at[2], to).start()
+
     got(kg_fwd.at[0], kg_rsem.at[2])
     got(kg_half.at[0], kg_rsem.at[0])
     kg_src[2, pl.ds(0, 64)] = kg_src[2, pl.ds(0, 64)] + kg_fwd[0, pl.ds(0, 64)] + kg_half[0]
@@ -434,21 +456,14 @@
     kg_src[6, pl.ds(64, 64)] = kg_src[6, pl.ds(64, 64)] + kg_fwd[1, pl.ds(64, 64)] + kg_half[1]
     remote(kg_src.at[6], kg_y.at[3], kg_ssem.at[7], kg_rsem.at[7], down2).start()
 
-    got(l_xc.at[pl.ds(0, 7)], l_rsem.at[0])
-    l_z[z] = add_slots(l_xc)
-    for to in z_ids:
-        remote(l_z.at[z], l_z.at[z], l_ssem.at[1], l_rsem.at[1], to).start()
-
     at = pl.ds(pl.multiple_of(zl * 128, 128), 128)
-    part = ab_rows[0, c, :, at] * q_end(0) - ab_rows[1, c, :, at] * q_end(1)
-    mine = fin.at[c, pl.ds(pl.multiple_of(x * 32, 32), 32)]
-    fin[c, pl.ds(pl.multiple_of(x * 32, 32), 32)] = part
-    for to in xc_ids:
-        remote(mine, mine, fin_ssem, fin_rsem, to).start()
-    got(l_z.at[pl.ds(0, 7)], l_rsem.at[1])
-    l_y[y] = add_slots(l_z)
-    for to in y_ids:
-        remote(l_y.at[y], l_y.at[y], l_ssem.at[2], l_rsem.at[2], to).start()
+    for h in range(2):
+        part = ab_rows[0, c, :, at] * q_end(0, h) - ab_rows[1, c, :, at] * q_end(1, h)
+        feats = pl.ds(pl.multiple_of(x * 32 + h * 16, 16), 16)
+        mine = fin.at[c, feats]
+        fin[c, feats] = part
+        for to in xc_ids:
+            remote(mine, mine, fin_ssem.at[h], fin_rsem.at[h], to).start()
 
     part = kg_src[0]
     for i, k in ((0, 4), (1, 5), (2, 6), (3, 7)):
@@ -457,7 +472,8 @@
     own = pl.multiple_of((y * 8 + zl * NC + c) * 128, 128)
     pgrad_ref[...] = unit_back(kraw[pl.ds(own, 128)].astype(F32), part)
 
-    got(w_rcv.at[0], fin_rsem)
+    for h in range(2):
+        got(w_rcv.at[0, h], fin_rsem.at[h])
     for v in range(2):
         qt[v] = fin[v].T
     for v in range(2):
@@ -471,11 +487,11 @@
     sent(qg.at[0], gs_ssem)
     for it in range(3):
         sent(a_c.at[it], a_ssem.at[it, 0])
-        sent(a_pl.at[it], a_ssem.at[it, 1])
+        sent(a_pl.at[it, pl.ds(0, NP)], a_ssem.at[it, 1])
     for it in range(3):
         sent(b_y.at[it], b_ssem.at[it])
     sent(r_two.at[0], r_ssem.at[0])
-    sent(r_pl, r_ssem.at[1])
+    sent(r_pl.at[pl.ds(0, NP)], r_ssem.at[1])
     sent(cnt_y, cnt_ssem)
     for i in range(2):
         sent(kg_half.at[i], kg_ssem.at[i])
@@ -483,11 +499,13 @@
         sent(kg_y.at[i], kg_ssem.at[4 + i])
         sent(kg_y.at[2 + i], kg_ssem.at[6 + i])
         sent(c_rcv.at[i], f_ssem.at[i, 0])
-        sent(x_rcv.at[i], f_ssem.at[i, 1])
-        sent(w_rcv.at[i], f_ssem.at[i, 2])
-    sent(w_rcv.at[0], fin_ssem)
-    for i in range(3):
-        sent(l_xc.at[pl.ds(0, 7)], l_ssem.at[i])
+        for h in range(2):
+            sent(x_rcv.at[i, h], f_ssem.at[i, 1 + h])
+            sent(w_rcv.at[i, h], f_ssem.at[i, 3 + h])
+        sent(w_rcv.at[0, i], fin_ssem.at[i])
+    sent(x_c, l_ssem.at[0])
+    sent(x_pl.at[pl.ds(0, NP)], l_ssem.at[1])
+    sent(l_y.at[pl.ds(0, 7)], l_ssem.at[2])
 
 
 def hand_on(view_in, pgrad_in, loss_in, view_ref, pgrad_ref, loss_ref):
@@ -517,14 +535,13 @@
         vmem((2, 512, 1024), BF16),
         vmem((2, 1024, 512), F32),
         vmem((2048, 512), BF16),
-        vmem((3, 2, 1, 1024), F32),
         vmem((3, 1, 1024), F32),
-        vmem((3, NP, 1, 1024), F32),
+        vmem((3, 1, 1024), F32),
+        vmem((3, NP + 1, 1, 1024), F32),
         vmem((3, 1, 2048), F32),
         vmem((3, 7, 1, 2048), F32),
         vmem((2, 1, 256), F32),
-        vmem((NP, 2, 1, 256), F32),
-        vmem((4, 2, 1, 256), F32),
+        vmem((NP + 1, 2, 1, 256), F32),
         vmem((NGROUP, 128), F32),
         vmem((7, NGROUP, 128), F32),
         vmem((8, 128, FEAT), F32),
@@ -534,21 +551,21 @@
         vmem((2, FEAT, 512), F32),
         vmem((2, FEAT, 512), F32),
         vmem((2, FEAT, 512), F32),
-        vmem((2, 3, 32, 512), F32),
-        vmem((2, 4, 32, 128), F32),
-        vmem((2, 7, 32, 128), F32),
+        vmem((2, 2, 3, 16, 512), F32),
+        vmem((2, 2, 4, 16, 128), F32),
+        vmem((2, 2, 7, 16, 128), F32),
         vmem((2, FEAT, 128), F32),
         vmem((8, 1, 128), F32),
-        vmem((8, 1, 128), F32),
-        vmem((8, 1, 128), F32),
-        vmem((2, 1, 512), F32),
+        vmem((1, 1024), F32),
+        vmem((1, 1024), F32),
+        vmem((NP + 1, 1, 1024), F32),
         vmem((1, 2048), F32),
         vmem((2, 2, 1, 512), F32),
         vmem((2, 128, FEAT), F32),
         dma((2,)),
         dma, dma((3,)), dma, dma((4,)),
         dma((3, 2)), dma((3, 2)), dma((3,)), dma((3,)), dma((2,)), dma((2,)), dma, dma,
-        dma((8,)), dma((8,)), dma((2, 3)), dma((2, 3)), dma, dma, dma((3,)), dma((3,)),
+        dma((8,)), dma((8,)), dma((2, 5)), dma((2, 5)), dma((2,)), dma((2,)), dma((3,)), dma((3,)),
     ]
     view_grads, proto_grads, loss = pl.pallas_call(
         kernel,

time: 83.2 us -> 81.2 us (0.976); the launches traced: 81.7 us -> 81 us
  no operation moved by 1% of the time
where the time goes in v6:
time: 81.2 us; the launch traced here: 81 us
  Pallas kernels  80.4 us (99%)
    pallas_call x1, Pallas kernels, on_device(): pl.pallas_call(kernel, out_shape=(jax.ShapeDtypeStruct((2, 64, FEAT), F32...  78.2 us
    pallas_call x1, Pallas kernels, on_device(): pl.pallas_call(hand_on, out_shape=(jax.ShapeDtypeStruct((2, 64, FEAT), F3...  2.15 us

profile of v6, /device:TPU:1, one launch (start us, length us, event | category | flops | bytes accessed | tf_op | source)
XLA Modules:
  0.0 81.0 jit_solution(17032106473372175376)
XLA Ops:
  0.6 78.2 %swav_step.1 = (f32[2,64,128]{2,1,0:T(8,128)}, f32[128,128]{1,0:T(8,128)}, f32[1,1]{1,0:T(1,128)}) custom-call(bf16[2048,128]{1,0:T(8,128)(2,1)} %bitcast.3, s32[2,64]{1,0:T(2,128)} %off_ref.1, s32[1,64]{1,0:T(1,128)} %bitcast.4, bf16[8192,128]{1,0:T(8,128)(2,1)} %proto_ref.1), custom_call_target="tpu_custom_call" | custom-call | tf_op jit(solution)/shard_map/swav_step/pallas_call | solution.py:570
  78.8 2.2 %results.1 = (f32[2,64,128]{2,1,0:T(8,128)}, f32[128,128]{1,0:T(8,128)}, f32[1,1]{1,0:T(1,128)}) custom-call(f32[2,64,128]{2,1,0:T(8,128)} %get-tuple-element.9.view_in, f32[128,128]{1,0:T(8,128)} %get-tuple-element.10.pgrad_in, f32[1,1]{1,0:T(1,128)} %get-tuple-element.11.loss_in), custom_call_target="tpu_custom_call" | custom-call | tf_op jit(solution)/shard_map/results/pallas_call | solution.py:590

commit v7 on v6

--- a/solution.py
+++ b/solution.py
@@ -136,16 +136,12 @@
 
     load_key.wait()
 
-    def normalise(i, carry):
-        at = pl.ds(pl.multiple_of(i * 2048, 2048), 2048)
-        raw = kraw[at].astype(F32)
-        kunit[at] = (raw * (unit_scale(raw) * (1.0 / math.sqrt(FEAT)))).astype(BF16)
-        return carry
-
-    lax.fori_loop(0, 4, normalise, 0)
     def whole(i, sums):
         at = pl.ds(pl.multiple_of(i * 4096, 4096), 4096)
-        e = jnp.exp(mm(kunit[at], query, NT) * 10.0)
+        raw = kraw[at].astype(F32)
+        unit = (raw * (unit_scale(raw) * (1.0 / math.sqrt(FEAT)))).astype(BF16)
+        kunit[at] = unit
+        e = jnp.exp(mm(unit, query, NT) * 10.0)
         k = (e * e).astype(BF16).astype(F32)
         fold = lambda a: jnp.sum(a.reshape(512, 8, 128), axis=0)
         return sums[0] + fold(k), sums[1] + fold(e)
@@ -196,17 +192,16 @@
     got(qg.at[1 - c, zl], gs_rsem.at[0])
     scores(zl)
 
-    def member(i, step):
-        zp = lax.rem(zl + step, NZL)
-        piece = qg.at[c, zp]
+    steps = ((1, 3), (2, 1), (0, 2))
+    for i, step in steps:
+        piece = qg.at[c, lax.rem(zl + step, NZL)]
         got(piece, g_rsem.at[i])
         remote(piece, piece, gs_ssem, gs_rsem.at[i + 1], sib).start()
+    for i, step in steps:
+        zp = lax.rem(zl + step, NZL)
         got(qg.at[1 - c, zp], gs_rsem.at[i + 1])
         scores(zp)
 
-    member(1, 3)
-    member(2, 1)
-    member(0, 2)
     got(r_pl.at[pl.ds(0, NP)], r_rsem.at[1])
     pairs = []
     for j in range(NZL):

time: 81.2 us -> 80.1 us (0.986)
  Pallas kernels: 80.4 us -> 79.3 us
    pallas_call x1, Pallas kernels: 78.2 us -> 77.1 us  [on_device(): pl.pallas_call(kernel, out_shape=(jax.ShapeDtypeStruct((2, 64, FEAT), F32...]
where the time goes in v7:
time: 80.1 us; the launch traced here: 79.9 us
  Pallas kernels  79.3 us (99%)
    pallas_call x1, Pallas kernels, on_device(): pl.pallas_call(kernel, out_shape=(jax.ShapeDtypeStruct((2, 64, FEAT), F32...  77.1 us
    pallas_call x1, Pallas kernels, on_device(): pl.pallas_call(hand_on, out_shape=(jax.ShapeDtypeStruct((2, 64, FEAT), F3...  2.15 us

profile of v7, /device:TPU:1, one launch (start us, length us, event | category | flops | bytes accessed | tf_op | source)
XLA Modules:
  0.0 79.9 jit_solution(2560354260624467030)
XLA Ops:
  0.6 77.1 %swav_step.1 = (f32[2,64,128]{2,1,0:T(8,128)}, f32[128,128]{1,0:T(8,128)}, f32[1,1]{1,0:T(1,128)}) custom-call(bf16[2048,128]{1,0:T(8,128)(2,1)} %bitcast.3, s32[2,64]{1,0:T(2,128)} %off_ref.1, s32[1,64]{1,0:T(1,128)} %bitcast.4, bf16[8192,128]{1,0:T(8,128)(2,1)} %proto_ref.1), custom_call_target="tpu_custom_call" | custom-call | tf_op jit(solution)/shard_map/swav_step/pallas_call | solution.py:565
  77.8 2.2 %results.1 = (f32[2,64,128]{2,1,0:T(8,128)}, f32[128,128]{1,0:T(8,128)}, f32[1,1]{1,0:T(1,128)}) custom-call(f32[2,64,128]{2,1,0:T(8,128)} %get-tuple-element.9.view_in, f32[128,128]{1,0:T(8,128)} %get-tuple-element.10.pgrad_in, f32[1,1]{1,0:T(1,128)} %get-tuple-element.11.loss_in), custom_call_target="tpu_custom_call" | custom-call | tf_op jit(solution)/shard_map/results/pallas_call | solution.py:585

commit v8 on v7

--- a/solution.py
+++ b/solution.py
@@ -379,23 +379,25 @@
         remote(x_own, x_c, l_ssem.at[0], l_rsem.at[0], sib).start()
         got(x_c, l_rsem.at[0])
         cross_sum.append(plane_sum(x_own[...] + x_c[...], x_pl, l_ssem.at[1], l_rsem.at[1], nothing))
-
-    cross_sum = []
+        got(cnt_y, cnt_rsem)
+        counts = cnt_src[...]
+        for i in range(7):
+            counts = counts + cnt_y[i]
+        seen = jnp.sum(onehot * jnp.concatenate([counts] * 4, axis=1), axis=0, keepdims=True)
+        weight = WINDOWS / (NGROUP * seen)
+        tot_v = [totals[:, 0:512], totals[:, 512:1024]]
+        known.extend((weight, tot_v, [5.0 * weight / tot_v[v] for v in range(2)]))
+
+    cross_sum, known = [], []
     last = 1.0 / a_sum(2, lambda: q_theirs(1), beside_a2)
 
-    got(cnt_y, cnt_rsem)
-    counts = cnt_src[...]
-    for i in range(7):
-        counts = counts + cnt_y[i]
-    seen = jnp.sum(onehot * jnp.concatenate([counts] * 4, axis=1), axis=0, keepdims=True)
-    weight = WINDOWS / (NGROUP * seen)
+    weight, tot_v, a_v = known
     last_v = [last[:, 0:512], last[:, 512:1024]]
-    tot_v = [totals[:, 0:512], totals[:, 512:1024]]
-    a_v = [5.0 * weight / tot_v[v] for v in range(2)]
     b_v = [5.0 * weight * last_v[1 - v] for v in range(2)]
     for v in range(2):
         ab_rows[0, v] = a_v[v]
         ab_rows[1, v] = b_v[v]
+
     def add_slots(ref):
         out = ref[0]
         for i in range(1, 8):
@@ -564,16 +566,12 @@
     ]
     view_grads, proto_grads, loss = pl.pallas_call(
         kernel,
-        out_shape=(
-            jax.ShapeDtypeStruct((2, 64, FEAT), F32),
-            jax.ShapeDtypeStruct((128, FEAT), F32),
-            jax.ShapeDtypeStruct((1, 1), F32),
-        ),
+        out_shape=(vmem((2, 64, FEAT), F32), vmem((128, FEAT), F32), vmem((1, 1), F32)),
         in_specs=[anywhere, inside, inside, anywhere],
         out_specs=(inside, inside, inside),
         scratch_shapes=scratch,
         compiler_params=pltpu.CompilerParams(
-            collective_id=0, has_side_effects=True, vmem_limit_bytes=56 * 2**20
+            collective_id=0, has_side_effects=True, vmem_limit_bytes=60 * 2**20
         ),
         name="swav_step",
     )(
@@ -591,9 +589,9 @@
         ),
         in_specs=[inside] * 3,
         out_specs=(inside, inside, inside),
-        compiler_params=pltpu.CompilerParams(vmem_limit_bytes=60 * 2**20),
+        compiler_params=pltpu.CompilerParams(vmem_limit_bytes=16 * 2**20),
         name="results",
-    )(view_grads, proto_grads, loss)
+    )(*(pltpu.with_memory_space_constraint(a, pltpu.VMEM) for a in (view_grads, proto_grads, loss)))
     return view_grads, proto_grads, loss.reshape(())
 
 

time: 80.1 us -> 79 us (0.986)
  Pallas kernels: 79.3 us -> 78.2 us
    pallas_call x1, Pallas kernels: 2.15 us -> 1.3 us  [on_device(): pl.pallas_call(hand_on, out_shape=(jax.ShapeDtypeStruct((2, 64, FEAT), F3...]
where the time goes in v8:
time: 79 us; the launch traced here: 78.8 us
  Pallas kernels  78.2 us (99%)
    pallas_call x1, Pallas kernels, on_device(): pl.pallas_call(kernel, out_shape=(vmem((2, 64, FEAT), F32), vmem((128, FE...  76.9 us

profile of v8, /device:TPU:1, one launch (start us, length us, event | category | flops | bytes accessed | tf_op | source)
XLA Modules:
  0.0 78.8 jit_solution(14749312914239499504)
XLA Ops:
  0.6 76.9 %swav_step.1 = (f32[2,64,128]{2,1,0:T(8,128)S(1)}, f32[128,128]{1,0:T(8,128)S(1)}, f32[1,1]{1,0:T(1,128)}) custom-call(bf16[2048,128]{1,0:T(8,128)(2,1)} %bitcast.3, s32[2,64]{1,0:T(2,128)} %off_ref.1, s32[1,64]{1,0:T(1,128)} %bitcast.4, bf16[8192,128]{1,0:T(8,128)(2,1)} %proto_ref.1), custom_call_target="tpu_custom_call" | custom-call | tf_op jit(solution)/shard_map/swav_step/pallas_call | solution.py:567
  77.5 1.3 %results.1 = (f32[2,64,128]{2,1,0:T(8,128)}, f32[128,128]{1,0:T(8,128)}, f32[1,1]{1,0:T(1,128)}) custom-call(f32[2,64,128]{2,1,0:T(8,128)S(1)} %get-tuple-element.9.view_in, f32[128,128]{1,0:T(8,128)S(1)} %get-tuple-element.10.pgrad_in, f32[1,1]{1,0:T(1,128)} %get-tuple-element.11.loss_in), custom_call_target="tpu_custom_call" | custom-call | tf_op jit(solution)/shard_map/results/pallas_call | solution.py:583

commit v9 on v8

--- a/solution.py
+++ b/solution.py
@@ -422,15 +422,14 @@
     remote(kg_src.at[3], kg_fwd.at[0], kg_ssem.at[2], kg_rsem.at[2], up1).start()
     key_part(5, ahead(5))
     remote(kg_src.at[5], kg_fwd.at[1], kg_ssem.at[3], kg_rsem.at[3], down1).start()
-    key_part(2, ahead(2))
-    key_part(6, ahead(6))
     key_part(1, ahead(1))
     remote(kg_src.at[1], kg_y.at[0], kg_ssem.at[4], kg_rsem.at[4], up1).start()
     key_part(7, ahead(7))
     remote(kg_src.at[7], kg_y.at[1], kg_ssem.at[5], kg_rsem.at[5], down1).start()
+    q_z(1, 0)
+    key_part(2, ahead(2))
+    key_part(6, ahead(6))
     key_part(0, y)
-
-    q_z(1, 0)
     q_z(1, 1)
 
     shared = cross_sum[0]()

time: 79 us -> 78.7 us (level)
  no operation moved by 1% of the time
where the time goes in v9:
time: 78.7 us; the launch traced here: 78.6 us
  Pallas kernels  77.9 us (99%)
    pallas_call x1, Pallas kernels, on_device(): pl.pallas_call(kernel, out_shape=(vmem((2, 64, FEAT), F32), vmem((128, FE...  76.6 us

profile of v9, /device:TPU:1, one launch (start us, length us, event | category | flops | bytes accessed | tf_op | source)
XLA Modules:
  0.0 78.6 jit_solution(11079503520384316222)
XLA Ops:
  0.6 76.6 %swav_step.1 = (f32[2,64,128]{2,1,0:T(8,128)S(1)}, f32[128,128]{1,0:T(8,128)S(1)}, f32[1,1]{1,0:T(1,128)}) custom-call(bf16[2048,128]{1,0:T(8,128)(2,1)} %bitcast.3, s32[2,64]{1,0:T(2,128)} %off_ref.1, s32[1,64]{1,0:T(1,128)} %bitcast.4, bf16[8192,128]{1,0:T(8,128)(2,1)} %proto_ref.1), custom_call_target="tpu_custom_call" | custom-call | tf_op jit(solution)/shard_map/swav_step/pallas_call | solution.py:566
  77.3 1.3 %results.1 = (f32[2,64,128]{2,1,0:T(8,128)}, f32[128,128]{1,0:T(8,128)}, f32[1,1]{1,0:T(1,128)}) custom-call(f32[2,64,128]{2,1,0:T(8,128)S(1)} %get-tuple-element.9.view_in, f32[128,128]{1,0:T(8,128)S(1)} %get-tuple-element.10.pgrad_in, f32[1,1]{1,0:T(1,128)} %get-tuple-element.11.loss_in), custom_call_target="tpu_custom_call" | custom-call | tf_op jit(solution)/shard_map/results/pallas_call | solution.py:582

commit v10 on v9

--- a/solution.py
+++ b/solution.py
@@ -167,9 +167,6 @@
     for i in range(8):
         block = kunit[pl.ds(pl.multiple_of((i * 8 + zl * NC + c) * 128, 128), 128)]
         keys[pl.ds(i * 128, 128)] = block
-        turned = block.astype(F32).T.astype(BF16)
-        keys_t[:, pl.ds(i * 128, 128)] = turned
-        keys_t[:, pl.ds(1024 + i * 128, 128)] = turned
 
     def scores(zp):
         zp128 = pl.multiple_of(zp * 128, 128)
@@ -341,6 +338,10 @@
 
     def beside_a0():
         send_counts()
+        for i in range(8):
+            turned = keys[pl.ds(i * 128, 128)].astype(F32).T.astype(BF16)
+            keys_t[:, pl.ds(i * 128, 128)] = turned
+            keys_t[:, pl.ds(1024 + i * 128, 128)] = turned
         q_theirs(0)
         q_own(0)
 

time: 78.7 us -> 78.9 us (level)
  no operation moved by 1% of the time
where the time goes in v10:
time: 78.9 us; the launch traced here: 78.7 us
  Pallas kernels  78 us (99%)
    pallas_call x1, Pallas kernels, on_device(): pl.pallas_call(kernel, out_shape=(vmem((2, 64, FEAT), F32), vmem((128, FE...  76.7 us

profile of v10, /device:TPU:1, one launch (start us, length us, event | category | flops | bytes accessed | tf_op | source)
XLA Modules:
  0.0 78.7 jit_solution(1989799226405295911)
XLA Ops:
  0.6 76.7 %swav_step.1 = (f32[2,64,128]{2,1,0:T(8,128)S(1)}, f32[128,128]{1,0:T(8,128)S(1)}, f32[1,1]{1,0:T(1,128)}) custom-call(bf16[2048,128]{1,0:T(8,128)(2,1)} %bitcast.3, s32[2,64]{1,0:T(2,128)} %off_ref.1, s32[1,64]{1,0:T(1,128)} %bitcast.4, bf16[8192,128]{1,0:T(8,128)(2,1)} %proto_ref.1), custom_call_target="tpu_custom_call" | custom-call | tf_op jit(solution)/shard_map/swav_step/pallas_call | solution.py:567
  77.4 1.3 %results.1 = (f32[2,64,128]{2,1,0:T(8,128)}, f32[128,128]{1,0:T(8,128)}, f32[1,1]{1,0:T(1,128)}) custom-call(f32[2,64,128]{2,1,0:T(8,128)S(1)} %get-tuple-element.9.view_in, f32[128,128]{1,0:T(8,128)S(1)} %get-tuple-element.10.pgrad_in, f32[1,1]{1,0:T(1,128)} %get-tuple-element.11.loss_in), custom_call_target="tpu_custom_call" | custom-call | tf_op jit(solution)/shard_map/results/pallas_call | solution.py:583
